TPU v7x, 128 devices: a whole 4x4x4 slice. The times are simulated.
128 devices in a mesh: dp: 16 (over x_lo, z, core), space: 8 (over x_hi, y).
Axes of the slice: x: 4 (x_hi: 2, x_lo: 2; x = x_hi * 2 + x_lo), y: 4, z: 4, core: 2. Of those that a mesh axis runs over, the one named last changes fastest.
Arguments:
- features: bfloat16 [4096, 6272], P(('dp', 'space')), may hold values from -6 to 6
- grad_out: bfloat16 [4096, 6272], P(('dp', 'space')), may hold values from -6 to 6
- wigner: bfloat16 [455, 16384], P(None, ('dp', 'space')), may hold values from -1.5 to 1.5
- sources: int32 [16384], P(('dp', 'space')), may hold values from 0 to 47
- targets: int32 [16384], P(('dp', 'space')), may hold values from 0 to 31
- ghost_index: int32 [128, 2, 8], P(('dp', 'space')), may hold values from 0 to 31
- edge_count: int32 [16, 8], P('dp', 'space'), may hold values from 1 to 128, 768 in all within a row
- mixture: float32 [16, 32], replicated, may hold values from 0.25 to 2
- w_zero: bfloat16 [32, 896, 896], P('dp', 'space'), may hold values from -0.03125 to 0.03125
- w_one: bfloat16 [32, 2, 768, 768], P('dp', None, 'space'), may hold values from -0.02734375 to 0.02734375
- w_two: bfloat16 [32, 2, 640, 640], P('dp', None, 'space'), may hold values from -0.03125 to 0.03125
Outputs:
- updated: bfloat16 [4096, 6272], P(('dp', 'space'))
- grad_features: bfloat16 [4096, 6272], P(('dp', 'space'))
- grad_mix0: bfloat16 [16, 896, 896], P('dp', 'space')
- grad_mix1: bfloat16 [16, 2, 768, 768], P('dp', None, 'space')
- grad_mix2: bfloat16 [16, 2, 640, 640], P('dp', None, 'space')
Inputs may be any that keep to these rules, and one draw needn't show every extreme that they name: `edge_count`: the counts of one system sum to 768, and some device of every system has all 128 slots live.
All inputs are finite; a program needn't handle non-finite values.
Results may differ from a plain program's by a relative error of at most 0.015.
Values may be sent and summed in bfloat16 or wider, within the bound.
A program may use at most 128 MiB of HBM per device.

v0:
```python
import jax
import jax.numpy as jnp
from jax import lax
from jax.sharding import PartitionSpec as P

CHANNELS = 128
LMAX = 6
MMAX = 2


message_scale = 0.25


def with_halo(shard, sides, width):
    for axis, dim in sides:
        size, length = (lax.axis_size(axis), shard.shape[dim])
        up = [(i, (i + 1) % size) for i in range(size)]
        down = [(j, i) for i, j in up]
        last = lax.slice_in_dim(shard, length - width, length, axis=dim)
        initial = lax.slice_in_dim(shard, 0, width, axis=dim)
        before = lax.ppermute(last, axis, up)
        after = lax.ppermute(initial, axis, down)
        shard = jnp.concatenate([before, shard, after], axis=dim)
    return shard


def as_sent(shard):
    return jax.tree.map(lambda a: a.astype(jnp.bfloat16) if a.dtype == jnp.float32 else a, shard)


def degree_start(degree):
    return degree * (2 * degree - 1) * (2 * degree + 1) // 3


def rotate_into(wigner, edge_rows):
    row_count = edge_rows.shape[0]
    blocks = []
    for degree in range(LMAX + 1):
        extent = 2 * degree + 1
        kept_order = min(degree, MMAX)
        offset = degree_start(degree)
        matrix = wigner[offset : offset + extent * extent].reshape(extent, extent, row_count)[
            degree - kept_order : degree + kept_order + 1
        ]
        segment = edge_rows[
            :, degree * degree * CHANNELS : (degree + 1) * (degree + 1) * CHANNELS
        ].reshape(row_count, extent, CHANNELS)
        blocks.append(
            jnp.einsum("jne,enc->ejc", matrix, segment, preferred_element_type=jnp.float32).astype(
                jnp.bfloat16
            )
        )
    return blocks


def rotate_back(wigner, blocks):
    row_count = blocks[0].shape[0]
    pieces = []
    for degree in range(LMAX + 1):
        extent = 2 * degree + 1
        kept_order = min(degree, MMAX)
        offset = degree_start(degree)
        matrix = wigner[offset : offset + extent * extent].reshape(extent, extent, row_count)[
            degree - kept_order : degree + kept_order + 1
        ]
        pieces.append(
            jnp.einsum(
                "jne,ejc->enc", matrix, blocks[degree], preferred_element_type=jnp.float32
            ).reshape(row_count, extent * CHANNELS)
        )
    return jnp.concatenate(pieces, 1)


def split_frame(blocks):
    row_count = blocks[0].shape[0]
    frame_zero = jnp.stack([blocks[d][:, min(d, MMAX)] for d in range(LMAX + 1)], 1).reshape(
        row_count, -1
    )
    frame_pairs = []
    for order_m in range(1, MMAX + 1):
        plus_part = jnp.stack(
            [blocks[d][:, min(d, MMAX) + order_m] for d in range(order_m, LMAX + 1)], 1
        ).reshape(row_count, -1)
        minus_part = jnp.stack(
            [blocks[d][:, min(d, MMAX) - order_m] for d in range(order_m, LMAX + 1)], 1
        ).reshape(row_count, -1)
        frame_pairs.append((plus_part, minus_part))
    return (frame_zero, frame_pairs)


def join_frame(frame_zero, frame_pairs):
    row_count = frame_zero.shape[0]
    zero_rows = frame_zero.reshape(row_count, LMAX + 1, CHANNELS)
    reshaped = [
        (p.reshape(row_count, -1, CHANNELS), q.reshape(row_count, -1, CHANNELS))
        for p, q in frame_pairs
    ]
    blocks = []
    for degree in range(LMAX + 1):
        kept_order = min(degree, MMAX)
        row_list = []
        for order_m in range(-kept_order, kept_order + 1):
            if order_m == 0:
                row_list.append(zero_rows[:, degree])
            elif order_m > 0:
                row_list.append(reshaped[order_m - 1][0][:, degree - order_m])
            else:
                row_list.append(reshaped[-order_m - 1][1][:, degree + order_m])
        blocks.append(jnp.stack(row_list, 1))
    return blocks


def convolve(frame_zero, frame_pairs, mix_set):
    out_zero = jnp.dot(frame_zero, mix_set[0], preferred_element_type=jnp.float32).astype(
        jnp.bfloat16
    )
    out_pairs = []
    for index_m, (plus_part, minus_part) in enumerate(frame_pairs):
        real_weight = mix_set[index_m + 1][0]
        imag_weight = mix_set[index_m + 1][1]
        out_plus = jnp.dot(plus_part, real_weight, preferred_element_type=jnp.float32) - jnp.dot(
            minus_part, imag_weight, preferred_element_type=jnp.float32
        )
        out_minus = jnp.dot(plus_part, imag_weight, preferred_element_type=jnp.float32) + jnp.dot(
            minus_part, real_weight, preferred_element_type=jnp.float32
        )
        out_pairs.append((out_plus.astype(jnp.bfloat16), out_minus.astype(jnp.bfloat16)))
    return (out_zero, out_pairs)


def transposed(left_side, right_side):
    return lax.dot_general(
        left_side, right_side, (((1,), (1,)), ((), ())), preferred_element_type=jnp.float32
    )


def outer_product(left_side, right_side):
    return lax.dot_general(
        left_side, right_side, (((0,), (0,)), ((), ())), preferred_element_type=jnp.float32
    )


def convolve_back(frame_zero, frame_pairs, mix_set):
    grad_zero = transposed(frame_zero, mix_set[0]).astype(jnp.bfloat16)
    grad_pairs = []
    for index_m, (plus_part, minus_part) in enumerate(frame_pairs):
        real_weight = mix_set[index_m + 1][0]
        imag_weight = mix_set[index_m + 1][1]
        grad_plus = transposed(plus_part, real_weight) + transposed(minus_part, imag_weight)
        grad_minus = transposed(minus_part, real_weight) - transposed(plus_part, imag_weight)
        grad_pairs.append((grad_plus.astype(jnp.bfloat16), grad_minus.astype(jnp.bfloat16)))
    return (grad_zero, grad_pairs)


def weight_terms(frame_zero, frame_pairs, back_zero, back_pairs, weight_scale):
    result = [(weight_scale * outer_product(frame_zero, back_zero))[None]]
    for (plus_part, minus_part), (back_plus, back_minus) in zip(frame_pairs, back_pairs):
        real_grad = outer_product(plus_part, back_plus) + outer_product(minus_part, back_minus)
        imag_grad = outer_product(plus_part, back_minus) - outer_product(minus_part, back_plus)
        result.append(weight_scale * jnp.stack([real_grad, imag_grad]))
    return tuple(result)


def on_device(
    features,
    grad_out,
    wigner,
    sources,
    targets,
    ghost_index,
    edge_count,
    mixture,
    w_zero,
    w_one,
    w_two,
):
    own_rows = features.shape[0]
    edge_total = sources.shape[0]
    ghosts = ghost_index.shape[2]
    spaces = lax.axis_size("space")
    system = lax.axis_index("dp")
    per_group = w_zero.shape[0]
    cut_one = w_zero[0].size
    cut_two = cut_one + w_one[0].size
    local_flat = jnp.concatenate(
        [w_zero.reshape(per_group, -1), w_one.reshape(per_group, -1), w_two.reshape(per_group, -1)],
        1,
    )
    mix_row = lax.dynamic_index_in_dim(mixture, system, 0, keepdims=False)
    outgoing = jnp.concatenate([features[ghost_index[0, 1]], features[ghost_index[0, 0]]], 0)
    extended = with_halo(outgoing, (("space", 0),), ghosts)
    node_table = jnp.concatenate([features, extended[:ghosts], extended[3 * ghosts :]], 0)
    every_expert = lax.all_gather(local_flat, "dp", axis=0, tiled=True)
    grouped = every_expert.reshape(-1, per_group, every_expert.shape[1]).astype(jnp.float32)
    partial_mix = jnp.einsum(
        "ge,gep->gp", mix_row.reshape(-1, per_group), grouped, precision=lax.Precision.HIGHEST
    )
    rounded = lax.optimization_barrier(partial_mix.astype(jnp.bfloat16)).astype(jnp.float32)
    mixed_flat = jnp.sum(rounded, 0).astype(jnp.bfloat16)
    shard_zero = mixed_flat[:cut_one].reshape((1,) + w_zero.shape[1:])
    shard_one = mixed_flat[cut_one:cut_two].reshape(w_one.shape[1:])
    shard_two = mixed_flat[cut_two:].reshape(w_two.shape[1:])
    full_zero, full_one, full_two = (
        lax.all_gather(shard_zero, "space", axis=1, tiled=True),
        lax.all_gather(shard_one, "space", axis=1, tiled=True),
        lax.all_gather(shard_two, "space", axis=1, tiled=True),
    )
    mix_set = (full_zero[0], full_one, full_two)
    edge_rows = node_table[sources]
    frame_zero, frame_pairs = split_frame(rotate_into(wigner, edge_rows))
    out_zero, out_pairs = convolve(frame_zero, frame_pairs, mix_set)
    messages = rotate_back(wigner, join_frame(out_zero, out_pairs)).astype(jnp.bfloat16)
    is_live = jnp.arange(edge_total, dtype=jnp.int32) < edge_count[0, 0]
    target_hot = (
        (targets[None, :] == jnp.arange(own_rows, dtype=jnp.int32)[:, None]) & is_live[None, :]
    ).astype(jnp.bfloat16)
    gathered = jnp.dot(target_hot, messages, preferred_element_type=jnp.float32)
    updated = (features.astype(jnp.float32) + message_scale * gathered).astype(jnp.bfloat16)
    back_msg = (message_scale * outer_product(target_hot, grad_out)).astype(jnp.bfloat16)
    back_zero, back_pairs = split_frame(rotate_into(wigner, back_msg))
    grad_zero, grad_pairs = convolve_back(back_zero, back_pairs, mix_set)
    weight_scale = float(edge_total * spaces) ** (-0.5)
    partials = weight_terms(frame_zero, frame_pairs, back_zero, back_pairs, weight_scale)
    summed = jax.tree.map(
        lambda part: part.astype(jnp.float32),
        lax.psum_scatter(as_sent(partials), "space", scatter_dimension=1, tiled=True),
    )
    grad_mix0 = summed[0].astype(jnp.bfloat16)
    grad_mix1 = summed[1].astype(jnp.bfloat16)[None]
    grad_mix2 = summed[2].astype(jnp.bfloat16)[None]
    back_rows = rotate_back(wigner, join_frame(grad_zero, grad_pairs)).astype(jnp.bfloat16)
    source_hot = (
        sources[:, None] == jnp.arange(own_rows + 2 * ghosts, dtype=jnp.int32)[None, :]
    ).astype(jnp.bfloat16)
    table_grad = outer_product(source_hot, back_rows)
    returning = table_grad[own_rows:].astype(jnp.bfloat16)
    arriving = with_halo(returning, (("space", 0),), ghosts)
    prev_hot = (
        ghost_index[0, 1][:, None] == jnp.arange(own_rows, dtype=jnp.int32)[None, :]
    ).astype(jnp.bfloat16)
    next_hot = (
        ghost_index[0, 0][:, None] == jnp.arange(own_rows, dtype=jnp.int32)[None, :]
    ).astype(jnp.bfloat16)
    combined = grad_out.astype(jnp.float32) + table_grad[:own_rows]
    combined = (
        combined
        + outer_product(prev_hot, arriving[:ghosts])
        + outer_product(next_hot, arriving[3 * ghosts :])
    )
    grad_features = combined.astype(jnp.bfloat16)
    return (updated, grad_features, grad_mix0, grad_mix1, grad_mix2)


def solution(mesh):
    return jax.shard_map(
        on_device,
        mesh=mesh,
        in_specs=(
            P(("dp", "space"), None),
            P(("dp", "space"), None),
            P(None, ("dp", "space")),
            P(("dp", "space")),
            P(("dp", "space")),
            P(("dp", "space"), None, None),
            P("dp", "space"),
            P(),
            P("dp", "space", None),
            P("dp", None, "space", None),
            P("dp", None, "space", None),
        ),
        out_specs=(
            P(("dp", "space"), None),
            P(("dp", "space"), None),
            P("dp", "space", None),
            P("dp", None, "space", None),
            P("dp", None, "space", None),
        ),
        check_vma=False,
    )
```

profile of v0, /device:TPU:0, one launch (start us, length us, event | category | flops | bytes accessed | tf_op | source)
XLA Modules:
  0.0 654.6 jit_solution(16243563055059719981)
XLA Ops:
  8.6 1.7 copy.401
  10.6 19.5 %maximum_bitcast_fusion = bf16[1,2,350208]{2,1,0:T(2,128)(2,1)} fusion(bf16[2,102400]{1,0:T(2,128)(2,1)S(1)} %bitcast.317, bf16[2,147456]{1,0:T(2,128)(2,1)S(1)} %bitcast.308, bf16[2,100352]{1,0:T(2,128)(2,1)S(1)} %bitcast.318), kind=kLoop, calls=%fused_computation.26 | loop fusion | flops 4202496 | bytes 2801664
  30.7 120.2 %all-gather.12.cloned.1.call-done = bf16[16,2,350208]{2,1,0:T(2,128)(2,1)} async-done(((bf16[1,2,350208]{2,1,0:T(2,128)(2,1)}), bf16[16,2,350208]{2,1,0:T(2,128)(2,1)}) %all-gather.12.cloned.1.call-update) | async-done | bytes 22413328 | tf_op jit(solution)/shard_map/all_gather | solution.py:193
  150.9 77.1 %fusion.108 = bf16[16,1,350208]{2,1,0:T(2,128)(2,1)} fusion(f32[16,2,1]{1,2,0:T(1,128)S(1)} %bitcast.358, bf16[16,2,350208]{2,1,0:T(2,128)(2,1)} %all-gather.12.cloned.1.call-done), kind=kOutput, calls=%fused_computation.216 | convolution fusion | flops 134479872 | bytes 33620096 | tf_op jit(solution)/shard_map/ge,gep->gp/dot_general | solution.py:195
  228.0 17.0 %copy.422 = bf16[16,1,350208]{2,0,1:T(8,128)(2,1)} copy(bf16[16,1,350208]{2,1,0:T(2,128)(2,1)} %fusion.108) | data formatting | bytes 22413312 | tf_op jit(solution)/shard_map/ge,gep->gp/dot_general | solution.py:195
  245.0 15.5 %reduce_sum.12 = bf16[350208]{0:T(1024)(128)(2,1)S(1)} reduce(bf16[16,350208]{1,0:T(8,128)(2,1)} %bitcast.275, bf16[]{:T(256)} %constant.6.clone.1), dimensions={0}, to_apply=%region_0.1 | reduce | flops 5253120 | bytes 11907074 | tf_op jit(solution)/shard_map/reduce_sum | solution.py:199
  262.8 5.2 collective-permute-start.1
  283.3 2.2 copy.285
  295.9 2.0 copy.288
  323.3 1.7 fusion.11
  338.5 1.9 fusion.5
  340.4 2.9 fusion.21
  343.4 1.8 copy.289
  348.2 2.1 fusion.18
  363.4 1.7 fusion.48
  365.1 2.2 fusion.37
  367.2 1.7 copy.226
  403.3 17.5 %all-gather.8.cloned.1.call-done = bf16[2,768,768]{2,1,0:T(8,128)(2,1)} async-done(((bf16[2,96,768]{2,1,0:T(8,128)(2,1)}), bf16[2,768,768]{2,1,0:T(8,128)(2,1)}) %all-gather.8.cloned.1.call-update) | async-done | bytes 2359312 | tf_op jit(solution)/shard_map/all_gather | solution.py:205
  422.5 2.5 fusion.25
  425.0 1.7 copy.220
  432.1 1.7 copy.217
  445.9 2.0 stack.92
  447.8 2.2 fusion.12
  453.0 2.0 stack.93
  454.9 2.1 fusion.13
  460.1 2.1 stack.94
  462.2 2.2 fusion.14
  467.1 1.7 copy.296
  503.1 2.4 fusion.107
  511.3 5.2 collective-permute-done.2
  517.7 50.6 %reduce-scatter.8.cloned.1.call-done = bf16[2,80,640]{2,1,0:T(8,128)(2,1)} async-done(((bf16[2,640,640]{2,1,0:T(8,128)(2,1)}), bf16[2,80,640]{2,1,0:T(8,128)(2,1)}) %reduce-scatter.8.cloned.1.call-update) | async-done | bytes 204816 | tf_op jit(solution)/shard_map/reduce_scatter | solution.py:226
  568.2 79.3 %reduce-scatter.6.cloned.1.call-done = bf16[2,96,768]{2,1,0:T(8,128)(2,1)} async-done(((bf16[2,768,768]{2,1,0:T(8,128)(2,1)}), bf16[2,96,768]{2,1,0:T(8,128)(2,1)}) %reduce-scatter.6.cloned.1.call-update) | async-done | bytes 294928 | tf_op jit(solution)/shard_map/reduce_scatter | solution.py:226
  (539 shorter events, 185.9 us)
Async XLA Ops:
  7.2 23.5 %copy-start = (f32[16,32]{1,0:T(8,128)S(1)}, f32[16,32]{1,0:T(8,128)}, u32[]{:S(2)}) copy-start(f32[16,32]{1,0:T(8,128)} %param.18) | copy-start | bytes 6148
  7.2 143.7 %all-gather.12.cloned.1.call-start = ((), (), s32[]{:S(2)}) async-start(), calls=%async_computation.9 | async-start | bytes 23814144 | tf_op jit(solution)/shard_map/all_gather | solution.py:193
  30.1 310.3 %all-gather.6.cloned.1.call-start = ((), (), s32[]{:S(2)}) async-start(), calls=%async_computation.3 | async-start | bytes 1806336 | tf_op jit(solution)/shard_map/all_gather | solution.py:204
  245.0 16.6 %copy-start.110 = (s32[1,2,8]{2,1,0:T(2,128)S(1)}, s32[1,2,8]{2,1,0:T(2,128)}, u32[]{:S(2)}) copy-start(s32[1,2,8]{2,1,0:T(2,128)} %param.16) | copy-start | bytes 196
  245.0 16.6 %copy-start.4 = (bf16[32,6272]{1,0:T(8,128)(2,1)S(1)}, bf16[32,6272]{1,0:T(8,128)(2,1)}, u32[]{:S(2)}) copy-start(bf16[32,6272]{1,0:T(8,128)(2,1)} %param.11) | copy-start | bytes 1204228
  260.5 10.3 %copy-start.17 = (bf16[350208]{0:T(1024)(128)(2,1)}, bf16[350208]{0:T(1024)(128)(2,1)S(1)}, u32[]{:S(2)}) copy-start(bf16[350208]{0:T(1024)(128)(2,1)S(1)} %reduce_sum.12) | copy-start | bytes 2101252
  260.5 10.5 %copy-start.32 = (bf16[32,6272]{1,0:T(8,128)(2,1)S(1)}, bf16[32,6272]{1,0:T(8,128)(2,1)}, u32[]{:S(2)}) copy-start(bf16[32,6272]{1,0:T(8,128)(2,1)} %param.12) | copy-start | bytes 1204228
  260.5 10.5 %copy-start.112 = (s32[128]{0:T(128)S(1)}, s32[128]{0:T(128)}, u32[]{:S(2)}) copy-start(s32[128]{0:T(128)} %param.15) | copy-start | bytes 1540
  261.5 101.9 %all-gather.10.cloned.1.call-start = ((), (), s32[]{:S(2)}) async-start(), calls=%async_computation.5 | async-start | bytes 1843200 | tf_op jit(solution)/shard_map/all_gather | solution.py:206
  262.8 35.1 %collective-permute-start.1 = (bf16[8,6272]{1,0:T(8,128)(2,1)}, bf16[8,6272]{1,0:T(8,128)(2,1)}, u32[]{:S(2)}, u32[]{:S(2)}) collective-permute-start(bf16[8,6272]{1,0:T(8,128)(2,1)} %gather_fusion.1), channel_id=1, source_target_pairs={{1,0},{2,1},{3,2},{4,3},{5,4},{6,5},{7,6},{0,7},{9,8},{10,9},{11,1... | collective-permute-start | bytes 301064 | tf_op jit(solution)/shard_map/ppermute | solution.py:22
  269.3 28.7 %collective-permute-start = (bf16[8,6272]{1,0:T(8,128)(2,1)}, bf16[8,6272]{1,0:T(8,128)(2,1)}, u32[]{:S(2)}, u32[]{:S(2)}) collective-permute-start(bf16[8,6272]{1,0:T(8,128)(2,1)} %gather_fusion), channel_id=1, source_target_pairs={{0,1},{1,2},{2,3},{3,4},{4,5},{5,6},{6,7},{7,0},{8,9},{9,10},{10,1... | collective-permute-start | bytes 301064 | tf_op jit(solution)/shard_map/ppermute | solution.py:21
  270.8 150.0 %all-gather.8.cloned.1.call-start = ((), (), s32[]{:S(2)}) async-start(), calls=%async_computation.4 | async-start | bytes 2654208 | tf_op jit(solution)/shard_map/all_gather | solution.py:205
  285.8 7.8 %slice-start.8 = ((bf16[350208]{0:T(1024)(128)(2,1)}), bf16[147456]{0:T(1024)(128)(2,1)S(1)}, s32[]{:S(2)}) async-start(bf16[350208]{0:T(1024)(128)(2,1)} %copy-done.17), calls=%async_computation.18 | async-start | bytes 589824 | tf_op jit(solution)/shard_map/slice | solution.py:201
  287.1 7.5 %copy-start.40 = (bf16[128,128,5]{1,0,2:T(8,128)(2,1)S(1)}, bf16[128,128,5]{1,0,2:T(8,128)(2,1)}, u32[]{:S(2)}) copy-start(bf16[128,128,5]{1,0,2:T(8,128)(2,1)} %copy.426) | copy-start | bytes 491524
  287.9 14.3 %copy-start.108 = (f32[128]{0:T(128)}, f32[128]{0:T(128)S(1)}, u32[]{:S(2)}) copy-start(f32[128]{0:T(128)S(1)} %bitcast_convert_fusion.1) | copy-start | bytes 1540
  290.7 7.3 %copy-start.118 = (s32[128]{0:T(128)S(1)}, s32[128]{0:T(128)}, u32[]{:S(2)}) copy-start(s32[128]{0:T(128)} %param.14) | copy-start | bytes 1540
  294.6 223.1 %reduce-scatter.4.cloned.1.call-start = ((), (), s32[]{:S(2)}) async-start(), calls=%async_computation.6 | async-start | bytes 1806336 | tf_op jit(solution)/shard_map/reduce_scatter | solution.py:226
  325.1 243.2 %reduce-scatter.8.cloned.1.call-start = ((), (), s32[]{:S(2)}) async-start(), calls=%async_computation.8 | async-start | bytes 1843200 | tf_op jit(solution)/shard_map/reduce_scatter | solution.py:226
  330.6 316.9 %reduce-scatter.6.cloned.1.call-start = ((), (), s32[]{:S(2)}) async-start(), calls=%async_computation.7 | async-start | bytes 2654208 | tf_op jit(solution)/shard_map/reduce_scatter | solution.py:226
  335.6 85.2 %copy-start.15 = (bf16[128,6,128]{0,2,1:T(8,128)(2,1)}, bf16[128,6,128]{0,2,1:T(8,128)(2,1)S(1)}, u32[]{:S(2)}) copy-start(bf16[128,6,128]{0,2,1:T(8,128)(2,1)S(1)} %copy.215) | copy-start | bytes 589828
  340.4 7.7 %copy-start.5 = (bf16[1,896,896]{2,1,0:T(8,128)(2,1)S(1)}, bf16[1,896,896]{2,1,0:T(8,128)(2,1)}, u32[]{:S(2)}) copy-start(bf16[1,896,896]{2,1,0:T(8,128)(2,1)} %all-gather.6.cloned.1.call-done) | copy-start | bytes 4816900
  350.3 8.1 %copy-start.92 = (bf16[128,1,128]{0,2,1:T(8,128)(2,1)S(1)}, bf16[128,1,128]{0,2,1:T(8,128)(2,1)}, u32[]{:S(2)}) copy-start(bf16[128,1,128]{0,2,1:T(8,128)(2,1)} %get-tuple-element.36) | copy-start | bytes 98308
  350.3 8.8 %copy-start.91 = (bf16[128,1,128]{0,2,1:T(8,128)(2,1)S(1)}, bf16[128,1,128]{0,2,1:T(8,128)(2,1)}, u32[]{:S(2)}) copy-start(bf16[128,1,128]{0,2,1:T(8,128)(2,1)} %get-tuple-element.35) | copy-start | bytes 98308
  350.3 9.6 %copy-start.90 = (bf16[128,1,128]{0,2,1:T(8,128)(2,1)S(1)}, bf16[128,1,128]{0,2,1:T(8,128)(2,1)}, u32[]{:S(2)}) copy-start(bf16[128,1,128]{0,2,1:T(8,128)(2,1)} %get-tuple-element.34) | copy-start | bytes 98308
  350.3 10.3 %copy-start.89 = (bf16[128,1,128]{0,2,1:T(8,128)(2,1)S(1)}, bf16[128,1,128]{0,2,1:T(8,128)(2,1)}, u32[]{:S(2)}) copy-start(bf16[128,1,128]{0,2,1:T(8,128)(2,1)} %get-tuple-element.33) | copy-start | bytes 98308
  363.4 8.5 %copy-start.3 = (bf16[2,640,640]{2,1,0:T(8,128)(2,1)S(1)}, bf16[2,640,640]{2,1,0:T(8,128)(2,1)}, u32[]{:S(2)}) copy-start(bf16[2,640,640]{2,1,0:T(8,128)(2,1)} %all-gather.10.cloned.1.call-done) | copy-start | bytes 4915204
  422.5 7.3 %copy-start.2 = (bf16[2,768,768]{2,1,0:T(8,128)(2,1)S(1)}, bf16[2,768,768]{2,1,0:T(8,128)(2,1)}, u32[]{:S(2)}) copy-start(bf16[2,768,768]{2,1,0:T(8,128)(2,1)} %all-gather.8.cloned.1.call-done) | copy-start | bytes 7077892
  505.5 5.4 collective-permute-start.3
  506.7 9.8 %copy-start.33 = (bf16[32,6272]{1,0:T(8,128)(2,1)S(1)}, bf16[32,6272]{1,0:T(8,128)(2,1)}, u32[]{:S(2)}) copy-start(bf16[32,6272]{1,0:T(8,128)(2,1)} %param.12) | copy-start | bytes 1204228
  506.7 9.7 %copy-start.116 = (s32[8]{0:T(128)S(1)}, s32[8]{0:T(128)}, u32[]{:S(2)}) copy-start(s32[8]{0:T(128)} %get-tuple-element.121) | copy-start | bytes 100
  508.2 8.3 %collective-permute-start.2 = (bf16[8,6272]{1,0:T(8,128)(2,1)S(1)}, bf16[8,6272]{1,0:T(8,128)(2,1)S(1)}, u32[]{:S(2)}, u32[]{:S(2)}) collective-permute-start(bf16[8,6272]{1,0:T(8,128)(2,1)S(1)} %get-tuple-element.5), channel_id=1, source_target_pairs={{0,1},{1,2},{2,3},{3,4},{4,5},{5,6},{6,7},{7,0},{8,9},{9,10},{10,1... | collective-permute-start | bytes 301064 | tf_op jit(solution)/shard_map/ppermute | solution.py:21
  510.9 136.6 %copy-start.1 = (f32[16,32]{1,0:T(8,128)S(1)}, f32[16,32]{1,0:T(8,128)}, u32[]{:S(2)}) copy-start(f32[16,32]{1,0:T(8,128)} %param.18) | copy-start | bytes 6148
  (108 other events, 344.0 us)
Sparse Core Ops, SparseCore 0:
  30.2 120.6 all-gather.11
  261.6 50.6 all-gather.5
  314.6 48.7 all-gather.9
  366.1 54.6 all-gather.7
  424.9 68.3 reduce-scatter.3
  497.9 70.2 reduce-scatter.7
  572.6 74.9 reduce-scatter.5
where the time goes:
time: 665 us; the launch traced here: 655 us
  waiting for transfers between devices  275 us (41%)
  local copies, waits for them, and re-layouts  178 us (27%)
  matrix products  134 us (20%)
  other arithmetic  41.8 us (6%)
  between operations  17.1 us (3%)
  starting transfers between devices  8.19 us (1%)
    reduce_scatter x3, waiting for transfers between devices, on_device(): lax.psum_scatter(as_sent(partials), 'space', scatter_dimension=1, tiled=T...  130 us
    all_gather x1, waiting for transfers between devices, on_device(): every_expert = lax.all_gather(local_flat, 'dp', axis=0, tiled=True)  120 us
    dot_general x1, matrix products, on_device(): jnp.einsum('ge,gep->gp', mix_row.reshape(-1, per_group), grouped, precisi...  77.1 us
    unnamed x318, local copies, waits for them, and re-layouts  73.7 us
    unnamed x2, other arithmetic  20.2 us
    all_gather x1, waiting for transfers between devices, on_device(): lax.all_gather(shard_one, 'space', axis=1, tiled=True)  17.5 us
    dot_general x1, local copies, waits for them, and re-layouts, on_device(): jnp.einsum('ge,gep->gp', mix_row.reshape(-1, per_group), grouped, precisi...  17 us
    reduce_sum x1, other arithmetic, on_device(): mixed_flat = jnp.sum(rounded, 0).astype(jnp.bfloat16)  15.5 us
  transfers between devices with their start and end apart: 11, of which 7 were waited for; matrix products, arithmetic and copies ran while one was open for 33% of the time, Pallas kernels for 0%

commit v1 on v0

v1 whole, which is shorter than its diff:
```python
import functools

import jax
import jax.numpy as jnp
from jax import lax
from jax.experimental import pallas as pl
from jax.experimental.pallas import tpu as pltpu
from jax.sharding import PartitionSpec as P

BF16 = jnp.bfloat16
F32 = jnp.float32
MESH = pl.DeviceIdType.MESH

LMAX = 6
MMAX = 2
EDGES = 128
ATOMS = 32
GHOSTS = 8
WIDTH = 6272
PACK = 3200
WIG = 455
MESSAGE_SCALE = 0.25
WEIGHT_SCALE = 1024.0 ** -0.5

ROWS = (112, 96, 80)
COLS = (896, 768, 640)
MATS = (1, 2, 2)
HALVES = (
    (0, 0, 0, 48, True),
    (0, 0, 48, 64, False),
    (1, 0, 0, 96, True),
    (1, 1, 0, 96, False),
    (2, 0, 0, 80, True),
    (2, 1, 0, 80, False),
)
COPIES = 128


def contract(left, right, left_dim, right_dim):
    return lax.dot_general(
        left, right, (((left_dim,), (right_dim,)), ((), ())), preferred_element_type=F32
    )


def whole(ref, chunk, lead):
    return ref.at[lead] if chunk == 0 else ref.at[(slice(None),) + lead]


def part(ref, half, lead):
    chunk, mat, first, rows, _ = half
    if chunk == 0:
        return ref.at[lead + (pl.ds(first, rows),)]
    return ref.at[(mat,) + lead]


def steps(count, body):
    def step(i, carry):
        body(i)
        return carry

    lax.fori_loop(0, count, step, 0)


def tiles16(i):
    return pl.ds(pl.multiple_of(i * 16, 16), 16)


def kernel(
    mixture, count, features, grad_out, wigner, sources, targets, ghost_col, ghost_row, w0, w1, w2,
    updated, grad_features, out0, out1, out2,
    raw0, raw1, raw2, par0, par1, par2, zf0, zf1, zf2, zl0, zl1, zl2, zr0, zr1, zr2,
    mix0, mix1, mix2, gw0, gw1, gw2, cf0, cf1, cf2, cl0, cl1, cl2, cr0, cr1, cr2,
    cs0, cs1, cs2, cx0, cx1, cx2,
    ghost_send, ghost_recv, back_send, back_recv,
    wig32, blk0, blk1, blk2, blk3, blk4, blk5, blk6,
    table, rows_f, rows_b, v0, v1, v2, d0, d1, d2, s1, s2, t0, t1, t2, u1, u2,
    table_own, table_ghost, send_sem, recv_sem,
):
    w = (w0, w1, w2)
    raw = (raw0, raw1, raw2)
    par = (par0, par1, par2)
    zf, zl, zr = (zf0, zf1, zf2), (zl0, zl1, zl2), (zr0, zr1, zr2)
    mix = (mix0, mix1, mix2)
    gw = (gw0, gw1, gw2)
    cf, cl, cr = (cf0, cf1, cf2), (cl0, cl1, cl2), (cr0, cr1, cr2)
    cs, cx = (cs0, cs1, cs2), (cx0, cx1, cx2)
    out = (out0, out1, out2)
    blocks = (blk0, blk1, blk2, blk3, blk4, blk5, blk6)

    dp, sp = lax.axis_index("dp"), lax.axis_index("space")
    core, z, xl = dp % 2, (dp // 2) % 4, dp // 8
    y, xh = sp % 4, sp // 4
    dp_core = dp + 1 - 2 * core
    dp_x = (1 - xl) * 8 + z * 2 + core
    dp_xc = (1 - xl) * 8 + z * 2 + 1 - core
    sp_x = (1 - xh) * 4 + y

    def at_z(step):
        return xl * 8 + ((z + step) % 4) * 2 + core

    def at_y(step):
        return xh * 4 + (y + step) % 4

    to_core, to_x = (dp_core, sp), (dp_x, sp)
    to_up, to_down = (at_z(1), sp), (at_z(3), sp)
    to_right, to_left = (dp, at_y(1)), (dp, at_y(3))
    to_far = (dp, sp_x)
    to_next, to_prev = (dp, (sp + 1) % 8), (dp, (sp + 7) % 8)
    partners = (to_core, to_x, to_up, to_down, to_right, to_left, to_far, to_next, to_prev)

    barrier = pltpu.get_barrier_semaphore()
    for partner in partners:
        pl.semaphore_signal(barrier, inc=1, device_id=partner, device_id_type=MESH)

    copies = []

    def send(source, target, device):
        index = len(copies)
        copy = pltpu.make_async_remote_copy(
            src_ref=source,
            dst_ref=target,
            send_sem=send_sem.at[index],
            recv_sem=recv_sem.at[index],
            device_id=device,
            device_id_type=MESH,
        )
        copy.start()
        copies.append(copy)
        return copy

    atom_lane = lax.broadcasted_iota(jnp.int32, (2 * GHOSTS, ATOMS), 1)
    pick = (atom_lane == ghost_col[...]).astype(BF16)
    ghosts = jnp.dot(pick, features[...], preferred_element_type=F32)
    for side in range(2):
        mine = ghosts[side * GHOSTS : (side + 1) * GHOSTS]
        ghost_send[side] = jnp.concatenate([mine[:, :PACK], mine[:, WIDTH - PACK :]], 0).astype(BF16)

    pl.semaphore_wait(barrier, len(partners))

    ghost_copies = [
        send(ghost_send.at[0], ghost_recv.at[0], to_next),
        send(ghost_send.at[1], ghost_recv.at[1], to_prev),
    ]
    raw_x, raw_core, raw_xc = {}, {}, {}
    for k in range(3):
        raw_x[k] = send(w[k], raw[k].at[1], to_x)
        raw_core[k] = send(w[k], raw[k].at[0], to_core)

    def forward_raw(k):
        raw_x[k].wait_recv()
        raw_xc[k] = send(raw[k].at[1], raw[k].at[2], to_core)

    z_first, z_direct, z_sum = {}, {}, {}

    def partials(k):
        raw_core[k].wait_recv()
        raw_xc[k].wait_recv()
        across = COLS[k] // 128
        scale = [
            [
                mixture[(xl * 4 + (z + step) % 4) * 2 + core, 2 * owner + i]
                for owner in (dp, dp_core, dp_x, dp_xc)
                for i in range(2)
            ]
            for step in range(4)
        ]
        for mat in range(MATS[k]):
            lead = () if k == 0 else (mat,)

            def body(t, mat=mat, lead=lead):
                rs = tiles16(t // across)
                c = pl.ds(pl.multiple_of((t % across) * 128, 128), 128)
                terms = [w[k][(i,) + lead + (rs, c)].astype(F32) for i in range(2)]
                for slot in range(3):
                    terms += [raw[k][(slot, i) + lead + (rs, c)].astype(F32) for i in range(2)]
                for step in range(4):
                    total = scale[step][0] * terms[0]
                    for factor, term in zip(scale[step][1:], terms[1:]):
                        total = total + factor * term
                    par[k][lead + (step, rs, c)] = total.astype(BF16)

            steps(ROWS[k] // 16 * across, body)
        for h, half in enumerate(HALVES):
            if half[0] != k:
                continue
            if half[4]:
                z_first[h] = send(part(par[k], half, (2,)), part(zf[k], half, ()), to_up)
                z_direct[h] = send(part(par[k], half, (3,)), part(zr[k], half, ()), to_down)
            else:
                z_first[h] = send(part(par[k], half, (2,)), part(zf[k], half, ()), to_down)
                z_direct[h] = send(part(par[k], half, (1,)), part(zl[k], half, ()), to_up)

    def add_into(target, extra, rows):
        def body(i):
            rs = tiles16(i)
            target[rs] = (target[rs].astype(F32) + extra[rs].astype(F32)).astype(BF16)

        steps(rows // 16, body)

    def relay_sums(k):
        for h, half in enumerate(HALVES):
            if half[0] != k:
                continue
            step = 1 if half[4] else 3
            z_first[h].wait_recv()
            add_into(part(par[k], half, (step,)), part(zf[k], half, ()), half[3])
            target = zl[k] if half[4] else zr[k]
            z_sum[h] = send(
                part(par[k], half, (step,)), part(target, half, ()), to_up if half[4] else to_down
            )

    b_far, b_right, b_left, b_relay = {}, {}, {}, {}

    def spread(k, own):
        place = xh if own else 1 - xh
        here = whole(mix[k], k, (place, y))
        b_right[k, own] = send(here, here, to_right)
        b_left[k, own] = send(here, here, to_left)

    def finish_mix(k):
        for h, half in enumerate(HALVES):
            if half[0] != k:
                continue
            z_direct[h].wait_recv()
            z_sum[h].wait_recv()
            own, up, down = (
                part(par[k], half, (0,)),
                part(zl[k], half, ()),
                part(zr[k], half, ()),
            )
            target = part(mix[k], half, (xh, y))

            def body(i, own=own, up=up, down=down, target=target):
                rs = tiles16(i)
                total = own[rs].astype(F32) + up[rs].astype(F32) + down[rs].astype(F32)
                target[rs] = total.astype(BF16)

            steps(half[3] // 16, body)
        here = whole(mix[k], k, (xh, y))
        b_far[k] = send(here, here, to_far)
        spread(k, True)

    xo = 1 - xh

    def spread_far(k):
        b_far[k].wait_recv()
        spread(k, False)

    def relay_mix(k, own):
        place = xh if own else xo
        b_right[k, own].wait_recv()
        b_left[k, own].wait_recv()
        for h, half in enumerate(HALVES):
            if half[0] != k:
                continue
            step = 3 if half[4] else 1
            here = part(mix[k], half, (place, (y + step) % 4))
            b_relay[h, own] = send(here, here, to_right if half[4] else to_left)

    c_first, c_direct, c_sum, c_far = {}, {}, {}, {}

    def weight_grads(k):
        rows = ROWS[k]
        for place in range(2):

            def body(b, place=place):
                rs = pl.ds(pl.multiple_of((place * 4 + b) * rows, 16), rows)
                if k == 0:
                    total = contract(v0[rs], d0[...], 1, 1)
                    gw0[place, b] = (WEIGHT_SCALE * total).astype(BF16)
                else:
                    left, right, swapped = ((v1, d1, s1), (v2, d2, s2))[k - 1]
                    left = left[rs]
                    real = contract(left, right[...], 1, 1)
                    gw[k][0, place, b] = (WEIGHT_SCALE * real).astype(BF16)
                    imag = contract(left, swapped[...], 1, 1)
                    gw[k][1, place, b] = (WEIGHT_SCALE * imag).astype(BF16)

            steps(4, body)
        for h, half in enumerate(HALVES):
            if half[0] != k:
                continue
            chunk, mat, first, rows, up = half

            def both(ref, step=None):
                lead = (slice(None),) if step is None else (slice(None), (y + step) % 4)
                if k == 0:
                    return ref.at[lead + (pl.ds(first, rows),)]
                return ref.at[(mat,) + lead]

            if up:
                c_first[h] = send(both(gw[k], 2), both(cf[k]), to_right)
                c_direct[h] = send(both(gw[k], 3), both(cr[k]), to_left)
            else:
                c_first[h] = send(both(gw[k], 2), both(cf[k]), to_left)
                c_direct[h] = send(both(gw[k], 1), both(cl[k]), to_right)

    def relay_grads(k):
        for h, half in enumerate(HALVES):
            if half[0] != k:
                continue
            chunk, mat, first, rows, up = half
            step = 1 if up else 3
            c_first[h].wait_recv()
            for place in range(2):
                add_into(
                    part(gw[k], half, (place, (y + step) % 4)), part(cf[k], half, (place,)), rows
                )
            target = cl[k] if up else cr[k]
            if k == 0:
                source = gw[k].at[:, (y + step) % 4, pl.ds(first, rows)]
                target = target.at[:, pl.ds(first, rows)]
            else:
                source = gw[k].at[mat, :, (y + step) % 4]
                target = target.at[mat]
            c_sum[h] = send(source, target, to_right if up else to_left)

    def halves_of(k, body):
        for half in HALVES:
            if half[0] == k:
                body(half)

    def sum_grads(k):
        for h, half in enumerate(HALVES):
            if half[0] == k:
                c_direct[h].wait_recv()
                c_sum[h].wait_recv()

        def one(half):
            terms = (
                part(gw[k], half, (xo, y)),
                part(cl[k], half, (xo,)),
                part(cr[k], half, (xo,)),
            )
            target = part(cs[k], half, ())

            def body(i):
                rs = tiles16(i)
                total = terms[0][rs].astype(F32) + terms[1][rs].astype(F32) + terms[2][rs].astype(F32)
                target[rs] = total.astype(BF16)

            steps(half[3] // 16, body)

        halves_of(k, one)
        c_far[k] = send(cs[k], cx[k], to_far)

    def finish_grads(k):
        c_far[k].wait_recv()

        def one(half):
            terms = (
                part(gw[k], half, (xh, y)),
                part(cl[k], half, (xh,)),
                part(cr[k], half, (xh,)),
                part(cx[k], half, ()),
            )
            target = part(out[k], half, (0,)) if k == 0 else out[k].at[0, half[1]]

            def body(i):
                rs = tiles16(i)
                total = terms[0][rs].astype(F32) + terms[1][rs].astype(F32)
                total = total + terms[2][rs].astype(F32) + terms[3][rs].astype(F32)
                target[rs] = total.astype(BF16)

            steps(half[3] // 16, body)

        halves_of(k, one)

    wig32[0:WIG] = wigner[...].astype(F32)
    for degree in range(LMAX + 1):
        extent, kept = 2 * degree + 1, min(degree, MMAX)
        start = degree * (2 * degree - 1) * (2 * degree + 1) // 3 + (degree - kept) * extent
        for j in range(2 * kept + 1):
            rows = wig32[start + j * extent : start + (j + 1) * extent]
            blocks[degree][j] = jnp.broadcast_to(rows[:, None, :], (extent, 8, EDGES))

    live = lax.broadcasted_iota(jnp.int32, (ATOMS, EDGES), 1) < count[0, 0]
    hot_target = (
        (lax.broadcasted_iota(jnp.int32, (ATOMS, EDGES), 0) == targets[...]) & live
    ).astype(F32)
    hot_quarter = (MESSAGE_SCALE * hot_target).astype(BF16)
    hot_target = hot_target.astype(BF16)
    hot_source = (
        lax.broadcasted_iota(jnp.int32, (ATOMS + 2 * GHOSTS, EDGES), 0) == sources[...]
    ).astype(BF16)

    def wide(i):
        return pl.ds(pl.multiple_of(i * 896, 128), 896)

    def back_gather(i):
        rows_b[wide(i)] = contract(grad_out[:, wide(i)], hot_quarter, 0, 0).astype(BF16)

    steps(7, back_gather)

    for copy in ghost_copies:
        copy.wait_recv()
    table[0:ATOMS] = features[...]
    came = [ghost_recv[side].astype(F32) for side in range(2)]
    for low, high, first, cut in ((0, PACK, 0, 0), (PACK, WIDTH, GHOSTS, 2 * PACK - WIDTH)):
        both = [a[first : first + GHOSTS, cut : cut + high - low] for a in came]
        table[ATOMS : ATOMS + 2 * GHOSTS, low:high] = jnp.concatenate(both, 0).astype(BF16)

    def gather(i):
        rows_f[wide(i)] = contract(table[:, wide(i)], hot_source, 0, 0).astype(BF16)

    steps(7, gather)

    def rotate_into(i):
        for source, f0, f1, f2 in ((rows_f, v0, v1, v2), (rows_b, d0, d1, d2)):
            for degree in range(LMAX + 1):
                kept = min(degree, MMAX)
                total = None
                for n in range(2 * degree + 1):
                    first = (degree * degree + n) * 128
                    row = source[pl.ds(pl.multiple_of(first + i * 16, 16), 16)].astype(F32)
                    factor = blocks[degree][:, n]
                    term = factor[:, None] * row.reshape(1, 2, 8, EDGES)
                    total = term if total is None else total + term
                result = total.reshape(2 * kept + 1, 16, EDGES).astype(BF16)
                f0[pl.ds(pl.multiple_of(degree * 128 + i * 16, 16), 16)] = result[kept]
                for order, target in ((1, f1), (2, f2)):
                    if kept >= order:
                        rs = pl.ds(pl.multiple_of((degree - order) * 128 + i * 16, 16), 16)
                        target[rs, 0:EDGES] = result[kept + order]
                        target[rs, EDGES : 2 * EDGES] = result[kept - order]

    steps(8, rotate_into)

    for source, target in ((d1, s1), (d2, s2)):
        target[:, 0:EDGES] = source[:, EDGES : 2 * EDGES]
        target[:, EDGES : 2 * EDGES] = -source[:, 0:EDGES]
    t0[...] = v0[...].T
    for source, target, swapped in ((v1, t1, u1), (v2, t2, u2)):
        target[...] = source[...].T
        swapped[0:EDGES] = -target[EDGES : 2 * EDGES]
        swapped[EDGES : 2 * EDGES] = target[0:EDGES]

    forward_raw(0)
    partials(0)
    weight_grads(0)
    relay_sums(0)
    weight_grads(2)
    finish_mix(0)
    forward_raw(1)
    partials(1)
    spread_far(0)
    relay_mix(0, True)
    weight_grads(1)
    relay_sums(1)
    relay_mix(0, False)
    finish_mix(1)
    forward_raw(2)
    partials(2)
    spread_far(1)
    relay_grads(0)
    relay_sums(2)
    relay_mix(1, True)
    finish_mix(2)
    relay_mix(1, False)
    relay_grads(2)
    spread_far(2)
    relay_mix(2, True)
    relay_grads(1)
    relay_mix(2, False)
    sum_grads(0)

    def convolve(k):
        for h, half in enumerate(HALVES):
            if half[0] == k:
                b_relay[h, True].wait_recv()
                b_relay[h, False].wait_recv()
        width = COLS[k]
        if k == 0:
            weight = mix0[...].reshape(width, width)
            v0[...] = jnp.dot(t0[...], weight, preferred_element_type=F32).T.astype(BF16)
            d0[...] = jnp.dot(weight, d0[...], preferred_element_type=F32).astype(BF16)
            return
        t, u, v, d, s = ((t1, u1, v1, d1, s1), (t2, u2, v2, d2, s2))[k - 1]
        real = mix[k][0].reshape(width, width)
        imag = mix[k][1].reshape(width, width)
        result = jnp.dot(t[...], real, preferred_element_type=F32)
        result = result + jnp.dot(u[...], imag, preferred_element_type=F32)
        v[...] = result.T.astype(BF16)
        result = jnp.dot(real, d[...], preferred_element_type=F32)
        d[...] = (result + jnp.dot(imag, s[...], preferred_element_type=F32)).astype(BF16)

    convolve(0)
    sum_grads(2)
    convolve(1)
    sum_grads(1)
    convolve(2)

    def rotate_back(target, f0, f1, f2):
        def body(i):
            for degree in range(LMAX + 1):
                extent, kept = 2 * degree + 1, min(degree, MMAX)
                rows = []
                for order in range(-kept, kept + 1):
                    source = (f0, f1, f2)[abs(order)]
                    rs = pl.ds(pl.multiple_of((degree - abs(order)) * 128 + i * 16, 16), 16)
                    lanes = slice(EDGES, 2 * EDGES) if order < 0 else slice(0, EDGES)
                    rows.append(source[rs, lanes].astype(F32).reshape(2, 8, EDGES))
                for n in range(extent):
                    total = None
                    for j, row in enumerate(rows):
                        term = blocks[degree][j, n][None] * row
                        total = term if total is None else total + term
                    first = (degree * degree + n) * 128
                    target[pl.ds(pl.multiple_of(first + i * 16, 16), 16)] = total.reshape(
                        16, EDGES
                    ).astype(BF16)

        steps(8, body)

    rotate_back(rows_b, d0, d1, d2)

    def scatter_back(i):
        total = contract(hot_source, rows_b[wide(i)], 1, 1)
        table_own[:, wide(i)] = total[0:ATOMS]
        table_ghost[:, wide(i)] = total[ATOMS : ATOMS + 2 * GHOSTS]

    steps(7, scatter_back)
    for side in range(2):
        mine = table_ghost[side * GHOSTS : (side + 1) * GHOSTS]
        back_send[side] = jnp.concatenate([mine[:, :PACK], mine[:, WIDTH - PACK :]], 0).astype(BF16)
    back_copies = [
        send(back_send.at[0], back_recv.at[0], to_prev),
        send(back_send.at[1], back_recv.at[1], to_next),
    ]

    rotate_back(rows_f, v0, v1, v2)

    def scatter(i):
        total = contract(hot_target, rows_f[wide(i)], 1, 1)
        updated[:, wide(i)] = (
            features[:, wide(i)].astype(F32) + MESSAGE_SCALE * total
        ).astype(BF16)

    steps(7, scatter)

    for k in (0, 2, 1):
        finish_grads(k)

    for copy in back_copies:
        copy.wait_recv()
    came = [back_recv[side].astype(F32) for side in range(2)]
    spots = (
        lax.broadcasted_iota(jnp.int32, (ATOMS, 2 * GHOSTS), 0) == ghost_row[...]
    ).astype(BF16)
    for low, high, first, cut in ((0, PACK, 0, 0), (PACK, WIDTH, GHOSTS, 2 * PACK - WIDTH)):
        both = [a[first : first + GHOSTS, cut : cut + high - low] for a in came]
        both = jnp.concatenate(both, 0).astype(BF16)
        total = grad_out[:, low:high].astype(F32) + table_own[:, low:high]
        total = total + jnp.dot(spots, both, preferred_element_type=F32)
        grad_features[:, low:high] = total.astype(BF16)

    for copy in copies:
        copy.wait_send()


def on_device(
    features, grad_out, wigner, sources, targets, ghost_index, edge_count, mixture,
    w_zero, w_one, w_two,
):
    def buffers(*lead):
        shapes = []
        for k in range(3):
            mats = () if k == 0 else (2,)
            shapes.append(pltpu.VMEM(mats + lead + (ROWS[k], COLS[k]), BF16))
        return shapes

    raw = [
        pltpu.VMEM((3, 2) + (() if k == 0 else (2,)) + (ROWS[k], COLS[k]), BF16) for k in range(3)
    ]
    frame = [
        pltpu.VMEM((896, EDGES), BF16),
        pltpu.VMEM((768, 2 * EDGES), BF16),
        pltpu.VMEM((640, 2 * EDGES), BF16),
    ]
    turned = [
        pltpu.VMEM((EDGES, 896), BF16),
        pltpu.VMEM((2 * EDGES, 768), BF16),
        pltpu.VMEM((2 * EDGES, 640), BF16),
    ]
    exchange = [pltpu.VMEM((2, 2 * GHOSTS, PACK), BF16)] * 4
    scratch = (
        raw
        + buffers(4)
        + buffers() * 3
        + buffers(2, 4)
        + buffers(2, 4)
        + buffers(2) * 3
        + buffers() * 2
        + exchange
        + [pltpu.VMEM((456, EDGES), F32)]
        + [
            pltpu.VMEM((2 * min(degree, MMAX) + 1, 2 * degree + 1, 8, EDGES), F32)
            for degree in range(LMAX + 1)
        ]
        + [pltpu.VMEM((ATOMS + 2 * GHOSTS, WIDTH), BF16)]
        + [pltpu.VMEM((WIDTH, EDGES), BF16)] * 2
        + frame * 2
        + frame[1:]
        + turned
        + turned[1:]
        + [pltpu.VMEM((ATOMS, WIDTH), F32), pltpu.VMEM((2 * GHOSTS, WIDTH), F32)]
        + [pltpu.SemaphoreType.DMA((COPIES,))] * 2
    )
    vmem = pl.BlockSpec(memory_space=pltpu.VMEM)
    smem = pl.BlockSpec(memory_space=pltpu.SMEM)
    return pl.pallas_call(
        kernel,
        out_shape=(
            jax.ShapeDtypeStruct((ATOMS, WIDTH), BF16),
            jax.ShapeDtypeStruct((ATOMS, WIDTH), BF16),
            jax.ShapeDtypeStruct((1, 112, 896), BF16),
            jax.ShapeDtypeStruct((1, 2, 96, 768), BF16),
            jax.ShapeDtypeStruct((1, 2, 80, 640), BF16),
        ),
        in_specs=[smem, smem] + [vmem] * 10,
        out_specs=(vmem,) * 5,
        scratch_shapes=scratch,
        compiler_params=pltpu.CompilerParams(
            collective_id=0, has_side_effects=True, vmem_limit_bytes=58 * 1024 * 1024
        ),
        name="message_layer",
    )(
        mixture,
        edge_count,
        features,
        grad_out,
        wigner,
        sources.reshape(1, -1),
        targets.reshape(1, -1),
        ghost_index.reshape(-1, 1),
        ghost_index.reshape(1, -1),
        w_zero,
        w_one,
        w_two,
    )


def solution(mesh):
    both = ("dp", "space")
    return jax.shard_map(
        on_device,
        mesh=mesh,
        in_specs=(
            P(both, None),
            P(both, None),
            P(None, both),
            P(both),
            P(both),
            P(both, None, None),
            P("dp", "space"),
            P(),
            P("dp", "space", None),
            P("dp", None, "space", None),
            P("dp", None, "space", None),
        ),
        out_specs=(
            P(both, None),
            P(both, None),
            P("dp", "space", None),
            P("dp", None, "space", None),
            P("dp", None, "space", None),
        ),
        check_vma=False,
    )
```

time: 665 us -> 142 us (0.21); the launches traced: 655 us -> 141 us
  waiting for transfers between devices: 275 us -> 0 us
  local copies, waits for them, and re-layouts: 178 us -> 7.59 us
  matrix products: 134 us -> 0 us
  Pallas kernels: 0 us -> 132 us
  other arithmetic: 41.8 us -> 0 us
  between operations: 17.1 us -> 1.31 us
  starting transfers between devices: 8.19 us -> 0 us
    all_gather x4 -> x0, waiting for transfers between devices: 138 us -> none  [the longest x1 120 us: on_device(): every_expert = lax.all_gather(local_flat, 'dp', axis=0, tiled=True)]
    dot_general x57 -> x0, matrix products: 134 us -> none  [the longest x1 77.1 us: on_device(): jnp.einsum('ge,gep->gp', mix_row.reshape(-1, per_group), grouped, precisi...]
    pallas_call x0 -> x1, Pallas kernels: none -> 132 us  [on_device(): pl.pallas_call(kernel, out_shape=(jax.ShapeDtypeStruct((ATOMS, WIDTH), BF...]
    reduce_scatter x3 -> x0, waiting for transfers between devices: 130 us -> none  [on_device(): lax.psum_scatter(as_sent(partials), 'space', scatter_dimension=1, tiled=T...]
    unnamed x318 -> x15, local copies, waits for them, and re-layouts: 73.7 us -> 6.33 us
    dot_general x19 -> x0, local copies, waits for them, and re-layouts: 28.5 us -> none  [the longest x1 17 us: on_device(): jnp.einsum('ge,gep->gp', mix_row.reshape(-1, per_group), grouped, precisi...]
    slice x65 -> x0, local copies, waits for them, and re-layouts: 22.9 us -> none  [the longest x32 8.44 us: rotate_into(): edge_rows[:, degree * degree * CHANNELS:(degree + 1) * (degree + 1) * CHA...]
    unnamed x2 -> x0, other arithmetic: 20.2 us -> none
  transfers between devices with their start and end apart: 11 -> 0, of which waited for: 7 -> 0; matrix products, arithmetic and copies ran while one was open for 33% -> 0% of each run, Pallas kernels for 0% -> 0%
where the time goes in v1:
time: 142 us; the launch traced here: 141 us
  Pallas kernels  132 us (93%)
  local copies, waits for them, and re-layouts  7.59 us (5%)
    pallas_call x1, Pallas kernels, on_device(): pl.pallas_call(kernel, out_shape=(jax.ShapeDtypeStruct((ATOMS, WIDTH), BF...  132 us
    unnamed x15, local copies, waits for them, and re-layouts  6.33 us

profile of v1, /device:TPU:0, one launch (start us, length us, event | category | flops | bytes accessed | tf_op | source)
XLA Modules:
  0.0 140.8 jit_solution(4357695979428413479)
XLA Ops:
  1.3 0.0 copy-start.4
  1.3 0.7 copy-done.4
  2.0 0.6 reshape.25.ghost_row
  2.5 0.7 reshape.26.ghost_col
  3.2 131.9 %message_layer.1 = (bf16[32,6272]{1,0:T(8,128)(2,1)}, bf16[32,6272]{1,0:T(8,128)(2,1)}, bf16[1,112,896]{2,1,0:T(8,128)(2,1)}, bf16[1,2,96,768]{3,2,1,0:T(8,128)(2,1)}, bf16[1,2,80,640]{3,2,1,0:T(8,128)(2,1)}) custom-call(f32[16,32]{1,0:T(8,128)} %mixture.1, s32[1,1]{1,0:T(1,128)S(6)} %copy.22.count, bf16[32,6272]{1,0:T(8,128)(2,1)} %features.1, ...), custom_call_target="tpu_custom_call" | custom-call | tf_op jit(solution)/shard_map/message_layer/pallas_call | solution.py:611
  135.1 0.0 copy-start
  135.1 1.8 %copy.23 = bf16[32,6272]{1,0:T(8,128)(2,1)} copy(bf16[32,6272]{1,0:T(8,128)(2,1)} %get-tuple-element.10) | data formatting | bytes 802816
  137.0 0.0 copy-done
  137.0 0.0 copy-start.3
  137.0 0.7 copy.24
  137.7 0.3 copy-done.3
  138.0 0.0 copy-start.1
  138.1 0.7 copy.25
  138.7 0.4 copy-done.1
  139.1 0.0 copy-start.2
  139.1 0.7 copy.26
  139.8 0.3 copy-done.2
  140.1 0.7 copy.27
Async XLA Ops:
  1.3 0.7 copy-start.4
  135.1 1.8 %copy-start = (bf16[32,6272]{1,0:T(8,128)(2,1)S(1)}, bf16[32,6272]{1,0:T(8,128)(2,1)}, u32[]{:S(2)}) copy-start(bf16[32,6272]{1,0:T(8,128)(2,1)} %get-tuple-element.11) | copy-start | bytes 1204228
  137.0 1.1 copy-start.3
  138.0 1.0 copy-start.1
  139.1 1.0 copy-start.2

commit v2 on v1

--- a/solution.py
+++ b/solution.py
@@ -18,7 +18,7 @@
 GHOSTS = 8
 WIDTH = 6272
 PACK = 3200
-WIG = 455
+WIG_READ = 416
 MESSAGE_SCALE = 0.25
 WEIGHT_SCALE = 1024.0 ** -0.5
 
@@ -70,10 +70,10 @@
     updated, grad_features, out0, out1, out2,
     raw0, raw1, raw2, par0, par1, par2, zf0, zf1, zf2, zl0, zl1, zl2, zr0, zr1, zr2,
     mix0, mix1, mix2, gw0, gw1, gw2, cf0, cf1, cf2, cl0, cl1, cl2, cr0, cr1, cr2,
-    cs0, cs1, cs2, cx0, cx1, cx2,
+    far_grad, far_wigner, hot_send, far_hot, far_v0, far_v1, far_v2,
     ghost_send, ghost_recv, back_send, back_recv,
-    wig32, blk0, blk1, blk2, blk3, blk4, blk5, blk6,
-    table, rows_f, rows_b, v0, v1, v2, d0, d1, d2, s1, s2, t0, t1, t2, u1, u2,
+    wig32, blk0, blk1, blk2, blk3, blk4, blk5, blk6, fbk0, fbk1, fbk2, fbk3, fbk4, fbk5, fbk6,
+    table, rows_f, rows_b, rows_p, v0, v1, v2, d0, d1, d2, p0, p1, p2, s1, s2, q1, q2, t0, t1, t2, u1, u2,
     table_own, table_ghost, send_sem, recv_sem,
 ):
     w = (w0, w1, w2)
@@ -83,9 +83,10 @@
     mix = (mix0, mix1, mix2)
     gw = (gw0, gw1, gw2)
     cf, cl, cr = (cf0, cf1, cf2), (cl0, cl1, cl2), (cr0, cr1, cr2)
-    cs, cx = (cs0, cs1, cs2), (cx0, cx1, cx2)
+    far_v = (far_v0, far_v1, far_v2)
     out = (out0, out1, out2)
     blocks = (blk0, blk1, blk2, blk3, blk4, blk5, blk6)
+    far_blocks = (fbk0, fbk1, fbk2, fbk3, fbk4, fbk5, fbk6)
 
     dp, sp = lax.axis_index("dp"), lax.axis_index("space")
     core, z, xl = dp % 2, (dp // 2) % 4, dp // 8
@@ -135,6 +136,18 @@
         mine = ghosts[side * GHOSTS : (side + 1) * GHOSTS]
         ghost_send[side] = jnp.concatenate([mine[:, :PACK], mine[:, WIDTH - PACK :]], 0).astype(BF16)
 
+    live = lax.broadcasted_iota(jnp.int32, (ATOMS, EDGES), 1) < count[0, 0]
+    hot_target = (
+        (lax.broadcasted_iota(jnp.int32, (ATOMS, EDGES), 0) == targets[...]) & live
+    ).astype(F32)
+    hot_quarter = (MESSAGE_SCALE * hot_target).astype(BF16)
+    hot_target = hot_target.astype(BF16)
+    hot_source = (
+        lax.broadcasted_iota(jnp.int32, (ATOMS + 2 * GHOSTS, EDGES), 0) == sources[...]
+    ).astype(BF16)
+
+    hot_send[...] = hot_quarter
+
     pl.semaphore_wait(barrier, len(partners))
 
     ghost_copies = [
@@ -142,9 +155,14 @@
         send(ghost_send.at[1], ghost_recv.at[1], to_prev),
     ]
     raw_x, raw_core, raw_xc = {}, {}, {}
+    far_copies = []
     for k in range(3):
         raw_x[k] = send(w[k], raw[k].at[1], to_x)
         raw_core[k] = send(w[k], raw[k].at[0], to_core)
+        if k == 0:
+            far_copies.append(send(grad_out, far_grad, to_far))
+            far_copies.append(send(wigner.at[0:WIG_READ], far_wigner, to_far))
+            far_copies.append(send(hot_send, far_hot, to_far))
 
     def forward_raw(k):
         raw_x[k].wait_recv()
@@ -257,132 +275,81 @@
             here = part(mix[k], half, (place, (y + step) % 4))
             b_relay[h, own] = send(here, here, to_right if half[4] else to_left)
 
-    c_first, c_direct, c_sum, c_far = {}, {}, {}, {}
+    c_first, c_direct, c_sum = {}, {}, {}
 
     def weight_grads(k):
         rows = ROWS[k]
-        for place in range(2):
-
-            def body(b, place=place):
-                rs = pl.ds(pl.multiple_of((place * 4 + b) * rows, 16), rows)
-                if k == 0:
-                    total = contract(v0[rs], d0[...], 1, 1)
-                    gw0[place, b] = (WEIGHT_SCALE * total).astype(BF16)
-                else:
-                    left, right, swapped = ((v1, d1, s1), (v2, d2, s2))[k - 1]
-                    left = left[rs]
-                    real = contract(left, right[...], 1, 1)
-                    gw[k][0, place, b] = (WEIGHT_SCALE * real).astype(BF16)
-                    imag = contract(left, swapped[...], 1, 1)
-                    gw[k][1, place, b] = (WEIGHT_SCALE * imag).astype(BF16)
-
-            steps(4, body)
+        far_rows[k].wait_recv()
+
+        def body(b):
+            own = pl.ds(pl.multiple_of((xh * 4 + b) * rows, 16), rows)
+            far = pl.ds(pl.multiple_of(b * rows, 16), rows)
+            if k == 0:
+                total = contract(v0[own], d0[...], 1, 1) + contract(far_v0[far], p0[...], 1, 1)
+                gw0[b] = (WEIGHT_SCALE * total).astype(BF16)
+            else:
+                v, d, s, p, q = ((v1, d1, s1, p1, q1), (v2, d2, s2, p2, q2))[k - 1]
+                mine, other = v[own], far_v[k][far]
+                real = contract(mine, d[...], 1, 1) + contract(other, p[...], 1, 1)
+                gw[k][0, b] = (WEIGHT_SCALE * real).astype(BF16)
+                imag = contract(mine, s[...], 1, 1) + contract(other, q[...], 1, 1)
+                gw[k][1, b] = (WEIGHT_SCALE * imag).astype(BF16)
+
+        steps(4, body)
         for h, half in enumerate(HALVES):
             if half[0] != k:
                 continue
-            chunk, mat, first, rows, up = half
-
-            def both(ref, step=None):
-                lead = (slice(None),) if step is None else (slice(None), (y + step) % 4)
-                if k == 0:
-                    return ref.at[lead + (pl.ds(first, rows),)]
-                return ref.at[(mat,) + lead]
-
-            if up:
-                c_first[h] = send(both(gw[k], 2), both(cf[k]), to_right)
-                c_direct[h] = send(both(gw[k], 3), both(cr[k]), to_left)
+
+            def block(step, half=half):
+                return part(gw[k], half, ((y + step) % 4,))
+
+            if half[4]:
+                c_first[h] = send(block(2), part(cf[k], half, ()), to_right)
+                c_direct[h] = send(block(3), part(cr[k], half, ()), to_left)
             else:
-                c_first[h] = send(both(gw[k], 2), both(cf[k]), to_left)
-                c_direct[h] = send(both(gw[k], 1), both(cl[k]), to_right)
+                c_first[h] = send(block(2), part(cf[k], half, ()), to_left)
+                c_direct[h] = send(block(1), part(cl[k], half, ()), to_right)
 
     def relay_grads(k):
         for h, half in enumerate(HALVES):
             if half[0] != k:
                 continue
-            chunk, mat, first, rows, up = half
-            step = 1 if up else 3
+            here = part(gw[k], half, ((y + (1 if half[4] else 3)) % 4,))
             c_first[h].wait_recv()
-            for place in range(2):
-                add_into(
-                    part(gw[k], half, (place, (y + step) % 4)), part(cf[k], half, (place,)), rows
-                )
-            target = cl[k] if up else cr[k]
-            if k == 0:
-                source = gw[k].at[:, (y + step) % 4, pl.ds(first, rows)]
-                target = target.at[:, pl.ds(first, rows)]
-            else:
-                source = gw[k].at[mat, :, (y + step) % 4]
-                target = target.at[mat]
-            c_sum[h] = send(source, target, to_right if up else to_left)
-
-    def halves_of(k, body):
-        for half in HALVES:
-            if half[0] == k:
-                body(half)
-
-    def sum_grads(k):
-        for h, half in enumerate(HALVES):
-            if half[0] == k:
-                c_direct[h].wait_recv()
-                c_sum[h].wait_recv()
-
-        def one(half):
-            terms = (
-                part(gw[k], half, (xo, y)),
-                part(cl[k], half, (xo,)),
-                part(cr[k], half, (xo,)),
-            )
-            target = part(cs[k], half, ())
-
-            def body(i):
-                rs = tiles16(i)
-                total = terms[0][rs].astype(F32) + terms[1][rs].astype(F32) + terms[2][rs].astype(F32)
-                target[rs] = total.astype(BF16)
-
-            steps(half[3] // 16, body)
-
-        halves_of(k, one)
-        c_far[k] = send(cs[k], cx[k], to_far)
+            add_into(here, part(cf[k], half, ()), half[3])
+            target = cl[k] if half[4] else cr[k]
+            c_sum[h] = send(here, part(target, half, ()), to_right if half[4] else to_left)
 
     def finish_grads(k):
-        c_far[k].wait_recv()
-
-        def one(half):
-            terms = (
-                part(gw[k], half, (xh, y)),
-                part(cl[k], half, (xh,)),
-                part(cr[k], half, (xh,)),
-                part(cx[k], half, ()),
+        for h, half in enumerate(HALVES):
+            if half[0] != k:
+                continue
+            c_direct[h].wait_recv()
+            c_sum[h].wait_recv()
+            own, left, right = (
+                part(gw[k], half, (y,)),
+                part(cl[k], half, ()),
+                part(cr[k], half, ()),
             )
             target = part(out[k], half, (0,)) if k == 0 else out[k].at[0, half[1]]
 
-            def body(i):
+            def body(i, own=own, left=left, right=right, target=target):
                 rs = tiles16(i)
-                total = terms[0][rs].astype(F32) + terms[1][rs].astype(F32)
-                total = total + terms[2][rs].astype(F32) + terms[3][rs].astype(F32)
+                total = own[rs].astype(F32) + left[rs].astype(F32) + right[rs].astype(F32)
                 target[rs] = total.astype(BF16)
 
             steps(half[3] // 16, body)
 
-        halves_of(k, one)
-
-    wig32[0:WIG] = wigner[...].astype(F32)
-    for degree in range(LMAX + 1):
-        extent, kept = 2 * degree + 1, min(degree, MMAX)
-        start = degree * (2 * degree - 1) * (2 * degree + 1) // 3 + (degree - kept) * extent
-        for j in range(2 * kept + 1):
-            rows = wig32[start + j * extent : start + (j + 1) * extent]
-            blocks[degree][j] = jnp.broadcast_to(rows[:, None, :], (extent, 8, EDGES))
-
-    live = lax.broadcasted_iota(jnp.int32, (ATOMS, EDGES), 1) < count[0, 0]
-    hot_target = (
-        (lax.broadcasted_iota(jnp.int32, (ATOMS, EDGES), 0) == targets[...]) & live
-    ).astype(F32)
-    hot_quarter = (MESSAGE_SCALE * hot_target).astype(BF16)
-    hot_target = hot_target.astype(BF16)
-    hot_source = (
-        lax.broadcasted_iota(jnp.int32, (ATOMS + 2 * GHOSTS, EDGES), 0) == sources[...]
-    ).astype(BF16)
+    def expand(matrix, target):
+        wig32[...] = matrix[0:WIG_READ].astype(F32)
+        for degree in range(LMAX + 1):
+            extent, kept = 2 * degree + 1, min(degree, MMAX)
+            start = degree * (2 * degree - 1) * (2 * degree + 1) // 3 + (degree - kept) * extent
+            for j in range(2 * kept + 1):
+                rows = wig32[start + j * extent : start + (j + 1) * extent]
+                target[degree][j] = jnp.broadcast_to(rows[:, None, :], (extent, 8, EDGES))
+
+    expand(wigner, blocks)
 
     def wide(i):
         return pl.ds(pl.multiple_of(i * 896, 128), 896)
@@ -405,15 +372,15 @@
 
     steps(7, gather)
 
-    def rotate_into(i):
-        for source, f0, f1, f2 in ((rows_f, v0, v1, v2), (rows_b, d0, d1, d2)):
+    def rotate_into(i, frames, matrices):
+        for source, f0, f1, f2 in frames:
             for degree in range(LMAX + 1):
                 kept = min(degree, MMAX)
                 total = None
                 for n in range(2 * degree + 1):
                     first = (degree * degree + n) * 128
                     row = source[pl.ds(pl.multiple_of(first + i * 16, 16), 16)].astype(F32)
-                    factor = blocks[degree][:, n]
+                    factor = matrices[degree][:, n]
                     term = factor[:, None] * row.reshape(1, 2, 8, EDGES)
                     total = term if total is None else total + term
                 result = total.reshape(2 * kept + 1, 16, EDGES).astype(BF16)
@@ -424,45 +391,67 @@
                         target[rs, 0:EDGES] = result[kept + order]
                         target[rs, EDGES : 2 * EDGES] = result[kept - order]
 
-    steps(8, rotate_into)
-
-    for source, target in ((d1, s1), (d2, s2)):
+    steps(8, lambda i: rotate_into(i, ((rows_f, v0, v1, v2), (rows_b, d0, d1, d2)), blocks))
+    far_rows = []
+    for k, source in enumerate((v0, v1, v2)):
+        rows = 4 * ROWS[k]
+        half = source.at[pl.ds(pl.multiple_of((1 - xh) * rows, 16), rows)]
+        far_rows.append(send(half, far_v[k], to_far))
+
+    def swap(source, target):
         target[:, 0:EDGES] = source[:, EDGES : 2 * EDGES]
         target[:, EDGES : 2 * EDGES] = -source[:, 0:EDGES]
+
+    swap(d1, s1)
+    swap(d2, s2)
     t0[...] = v0[...].T
     for source, target, swapped in ((v1, t1, u1), (v2, t2, u2)):
         target[...] = source[...].T
         swapped[0:EDGES] = -target[EDGES : 2 * EDGES]
         swapped[EDGES : 2 * EDGES] = target[0:EDGES]
 
+    def far_frame():
+        for copy in far_copies:
+            copy.wait_recv()
+        expand(far_wigner, far_blocks)
+        hot = far_hot[...]
+
+        def far_gather(i):
+            rows_p[wide(i)] = contract(far_grad[:, wide(i)], hot, 0, 0).astype(BF16)
+
+        steps(7, far_gather)
+        steps(8, lambda i: rotate_into(i, ((rows_p, p0, p1, p2),), far_blocks))
+        swap(p1, q1)
+        swap(p2, q2)
+
     forward_raw(0)
     partials(0)
-    weight_grads(0)
+    far_frame()
     relay_sums(0)
-    weight_grads(2)
     finish_mix(0)
     forward_raw(1)
+    weight_grads(0)
     partials(1)
     spread_far(0)
     relay_mix(0, True)
-    weight_grads(1)
     relay_sums(1)
     relay_mix(0, False)
     finish_mix(1)
     forward_raw(2)
+    weight_grads(1)
     partials(2)
     spread_far(1)
     relay_grads(0)
     relay_sums(2)
     relay_mix(1, True)
     finish_mix(2)
+    weight_grads(2)
     relay_mix(1, False)
-    relay_grads(2)
     spread_far(2)
     relay_mix(2, True)
     relay_grads(1)
     relay_mix(2, False)
-    sum_grads(0)
+    relay_grads(2)
 
     def convolve(k):
         for h, half in enumerate(HALVES):
@@ -484,10 +473,10 @@
         result = jnp.dot(real, d[...], preferred_element_type=F32)
         d[...] = (result + jnp.dot(imag, s[...], preferred_element_type=F32)).astype(BF16)
 
+    for copy in far_rows:
+        copy.wait_send()
     convolve(0)
-    sum_grads(2)
     convolve(1)
-    sum_grads(1)
     convolve(2)
 
     def rotate_back(target, f0, f1, f2):
@@ -538,7 +527,7 @@
 
     steps(7, scatter)
 
-    for k in (0, 2, 1):
+    for k in range(3):
         finish_grads(k)
 
     for copy in back_copies:
@@ -555,7 +544,8 @@
         grad_features[:, low:high] = total.astype(BF16)
 
     for copy in copies:
-        copy.wait_send()
+        if not any(copy is other for other in far_rows):
+            copy.wait_send()
 
 
 def on_device(
@@ -588,19 +578,28 @@
         + buffers(4)
         + buffers() * 3
         + buffers(2, 4)
-        + buffers(2, 4)
-        + buffers(2) * 3
-        + buffers() * 2
+        + buffers(4)
+        + buffers() * 3
+        + [
+            pltpu.VMEM((ATOMS, WIDTH), BF16),
+            pltpu.VMEM((WIG_READ, EDGES), BF16),
+            pltpu.VMEM((ATOMS, EDGES), BF16),
+            pltpu.VMEM((ATOMS, EDGES), BF16),
+            pltpu.VMEM((448, EDGES), BF16),
+            pltpu.VMEM((384, 2 * EDGES), BF16),
+            pltpu.VMEM((320, 2 * EDGES), BF16),
+        ]
         + exchange
-        + [pltpu.VMEM((456, EDGES), F32)]
+        + [pltpu.VMEM((WIG_READ, EDGES), F32)]
         + [
             pltpu.VMEM((2 * min(degree, MMAX) + 1, 2 * degree + 1, 8, EDGES), F32)
             for degree in range(LMAX + 1)
         ]
+        * 2
         + [pltpu.VMEM((ATOMS + 2 * GHOSTS, WIDTH), BF16)]
-        + [pltpu.VMEM((WIDTH, EDGES), BF16)] * 2
-        + frame * 2
-        + frame[1:]
+        + [pltpu.VMEM((WIDTH, EDGES), BF16)] * 3
+        + frame * 3
+        + frame[1:] * 2
         + turned
         + turned[1:]
         + [pltpu.VMEM((ATOMS, WIDTH), F32), pltpu.VMEM((2 * GHOSTS, WIDTH), F32)]

time: 142 us -> 150 us (1.056)
  Pallas kernels: 132 us -> 141 us
    pallas_call x1, Pallas kernels: 132 us -> 141 us  [on_device(): pl.pallas_call(kernel, out_shape=(jax.ShapeDtypeStruct((ATOMS, WIDTH), BF...]
where the time goes in v2:
time: 150 us
  Pallas kernels  141 us (94%)
  local copies, waits for them, and re-layouts  7.59 us (5%)
    pallas_call x1, Pallas kernels, on_device(): pl.pallas_call(kernel, out_shape=(jax.ShapeDtypeStruct((ATOMS, WIDTH), BF...  141 us
    unnamed x15, local copies, waits for them, and re-layouts  6.33 us

profile of v2, /device:TPU:0, one launch (start us, length us, event | category | flops | bytes accessed | tf_op | source)
XLA Modules:
  0.0 149.6 jit_solution(10263786445846635699)
XLA Ops:
  1.3 0.0 copy-start.4
  1.3 0.7 copy-done.4
  2.0 0.6 reshape.25.ghost_row
  2.5 0.7 reshape.26.ghost_col
  3.2 140.7 %message_layer.1 = (bf16[32,6272]{1,0:T(8,128)(2,1)}, bf16[32,6272]{1,0:T(8,128)(2,1)}, bf16[1,112,896]{2,1,0:T(8,128)(2,1)}, bf16[1,2,96,768]{3,2,1,0:T(8,128)(2,1)}, bf16[1,2,80,640]{3,2,1,0:T(8,128)(2,1)}) custom-call(f32[16,32]{1,0:T(8,128)} %mixture.1, s32[1,1]{1,0:T(1,128)S(6)} %copy.22.count, bf16[32,6272]{1,0:T(8,128)(2,1)} %features.1, ...), custom_call_target="tpu_custom_call" | custom-call | tf_op jit(solution)/shard_map/message_layer/pallas_call | solution.py:610
  143.9 0.0 copy-start
  143.9 1.8 %copy.23 = bf16[32,6272]{1,0:T(8,128)(2,1)} copy(bf16[32,6272]{1,0:T(8,128)(2,1)} %get-tuple-element.10) | data formatting | bytes 802816
  145.7 0.0 copy-done
  145.7 0.0 copy-start.3
  145.7 0.7 copy.24
  146.5 0.3 copy-done.3
  146.8 0.0 copy-start.1
  146.8 0.7 copy.25
  147.5 0.4 copy-done.1
  147.8 0.0 copy-start.2
  147.8 0.7 copy.26
  148.6 0.3 copy-done.2
  148.9 0.7 copy.27
Async XLA Ops:
  1.3 0.7 copy-start.4
  143.9 1.8 %copy-start = (bf16[32,6272]{1,0:T(8,128)(2,1)S(1)}, bf16[32,6272]{1,0:T(8,128)(2,1)}, u32[]{:S(2)}) copy-start(bf16[32,6272]{1,0:T(8,128)(2,1)} %get-tuple-element.11) | copy-start | bytes 1204228
  145.7 1.1 copy-start.3
  146.8 1.0 copy-start.1
  147.8 1.0 copy-start.2

commit v3 on v2

--- a/solution.py
+++ b/solution.py
@@ -25,13 +25,10 @@
 ROWS = (112, 96, 80)
 COLS = (896, 768, 640)
 MATS = (1, 2, 2)
-HALVES = (
-    (0, 0, 0, 48, True),
-    (0, 0, 48, 64, False),
-    (1, 0, 0, 96, True),
-    (1, 1, 0, 96, False),
-    (2, 0, 0, 80, True),
-    (2, 1, 0, 80, False),
+PARTS = (
+    ((0, 0, 48, True), (0, 48, 64, False)),
+    ((0, 0, 96, True), (1, 0, 96, False)),
+    ((0, 0, 80, True), (1, 0, 80, False)),
 )
 COPIES = 128
 
@@ -46,13 +43,6 @@
     return ref.at[lead] if chunk == 0 else ref.at[(slice(None),) + lead]
 
 
-def part(ref, half, lead):
-    chunk, mat, first, rows, _ = half
-    if chunk == 0:
-        return ref.at[lead + (pl.ds(first, rows),)]
-    return ref.at[(mat,) + lead]
-
-
 def steps(count, body):
     def step(i, carry):
         body(i)
@@ -68,8 +58,8 @@
 def kernel(
     mixture, count, features, grad_out, wigner, sources, targets, ghost_col, ghost_row, w0, w1, w2,
     updated, grad_features, out0, out1, out2,
-    raw0, raw1, raw2, par0, par1, par2, zf0, zf1, zf2, zl0, zl1, zl2, zr0, zr1, zr2,
-    mix0, mix1, mix2, gw0, gw1, gw2, cf0, cf1, cf2, cl0, cl1, cl2, cr0, cr1, cr2,
+    raw0, raw1, raw2, par0, par1, par2, za0, za1, za2, mix0, mix1, mix2,
+    keep0, keep1, keep2, cs0, cs1, cs2, cx0, cx1, cx2,
     far_grad, far_wigner, hot_send, far_hot, far_v0, far_v1, far_v2,
     ghost_send, ghost_recv, back_send, back_recv,
     wig32, blk0, blk1, blk2, blk3, blk4, blk5, blk6, fbk0, fbk1, fbk2, fbk3, fbk4, fbk5, fbk6,
@@ -79,10 +69,9 @@
     w = (w0, w1, w2)
     raw = (raw0, raw1, raw2)
     par = (par0, par1, par2)
-    zf, zl, zr = (zf0, zf1, zf2), (zl0, zl1, zl2), (zr0, zr1, zr2)
+    za = (za0, za1, za2)
     mix = (mix0, mix1, mix2)
-    gw = (gw0, gw1, gw2)
-    cf, cl, cr = (cf0, cf1, cf2), (cl0, cl1, cl2), (cr0, cr1, cr2)
+    keep, cs, cx = (keep0, keep1, keep2), (cs0, cs1, cs2), (cx0, cx1, cx2)
     far_v = (far_v0, far_v1, far_v2)
     out = (out0, out1, out2)
     blocks = (blk0, blk1, blk2, blk3, blk4, blk5, blk6)
@@ -103,11 +92,11 @@
         return xh * 4 + (y + step) % 4
 
     to_core, to_x = (dp_core, sp), (dp_x, sp)
-    to_up, to_down = (at_z(1), sp), (at_z(3), sp)
-    to_right, to_left = (dp, at_y(1)), (dp, at_y(3))
+    along_z = tuple((at_z(step), sp) for step in (1, 2, 3))
+    along_y = tuple((dp, at_y(step)) for step in (1, 2, 3))
     to_far = (dp, sp_x)
     to_next, to_prev = (dp, (sp + 1) % 8), (dp, (sp + 7) % 8)
-    partners = (to_core, to_x, to_up, to_down, to_right, to_left, to_far, to_next, to_prev)
+    partners = (to_core, to_x, to_far, to_next, to_prev) + along_z + along_y
 
     barrier = pltpu.get_barrier_semaphore()
     for partner in partners:
@@ -155,20 +144,23 @@
         send(ghost_send.at[1], ghost_recv.at[1], to_prev),
     ]
     raw_x, raw_core, raw_xc = {}, {}, {}
-    far_copies = []
+    grad_copies = []
     for k in range(3):
         raw_x[k] = send(w[k], raw[k].at[1], to_x)
         raw_core[k] = send(w[k], raw[k].at[0], to_core)
         if k == 0:
-            far_copies.append(send(grad_out, far_grad, to_far))
-            far_copies.append(send(wigner.at[0:WIG_READ], far_wigner, to_far))
-            far_copies.append(send(hot_send, far_hot, to_far))
+            for at in (0, 2):
+                grad_copies += [
+                    send(grad_out, far_grad.at[at], along_y[at]),
+                    send(wigner.at[0:WIG_READ], far_wigner.at[at], along_y[at]),
+                    send(hot_send, far_hot.at[at], along_y[at]),
+                ]
 
     def forward_raw(k):
         raw_x[k].wait_recv()
         raw_xc[k] = send(raw[k].at[1], raw[k].at[2], to_core)
 
-    z_first, z_direct, z_sum = {}, {}, {}
+    z_sums = {}
 
     def partials(k):
         raw_core[k].wait_recv()
@@ -198,147 +190,93 @@
                     par[k][lead + (step, rs, c)] = total.astype(BF16)
 
             steps(ROWS[k] // 16 * across, body)
-        for h, half in enumerate(HALVES):
-            if half[0] != k:
-                continue
-            if half[4]:
-                z_first[h] = send(part(par[k], half, (2,)), part(zf[k], half, ()), to_up)
-                z_direct[h] = send(part(par[k], half, (3,)), part(zr[k], half, ()), to_down)
-            else:
-                z_first[h] = send(part(par[k], half, (2,)), part(zf[k], half, ()), to_down)
-                z_direct[h] = send(part(par[k], half, (1,)), part(zl[k], half, ()), to_up)
-
-    def add_into(target, extra, rows):
+        z_sums[k] = [
+            send(whole(par[k], k, (at + 1,)), whole(za[k], k, (at,)), along_z[at]) for at in (0, 2, 1)
+        ]
+
+    def add_up(target, terms, rows, kind=BF16):
         def body(i):
             rs = tiles16(i)
-            target[rs] = (target[rs].astype(F32) + extra[rs].astype(F32)).astype(BF16)
+            total = terms[0][rs].astype(F32)
+            for term in terms[1:]:
+                total = total + term[rs].astype(F32)
+            target[rs] = total.astype(kind)
 
         steps(rows // 16, body)
 
-    def relay_sums(k):
-        for h, half in enumerate(HALVES):
-            if half[0] != k:
-                continue
-            step = 1 if half[4] else 3
-            z_first[h].wait_recv()
-            add_into(part(par[k], half, (step,)), part(zf[k], half, ()), half[3])
-            target = zl[k] if half[4] else zr[k]
-            z_sum[h] = send(
-                part(par[k], half, (step,)), part(target, half, ()), to_up if half[4] else to_down
-            )
-
-    b_far, b_right, b_left, b_relay = {}, {}, {}, {}
+    def matrix(ref, k, mat, lead):
+        return ref.at[lead] if k == 0 else ref.at[(mat,) + lead]
+
+    b_far, b_along = {}, {}
 
     def spread(k, own):
         place = xh if own else 1 - xh
         here = whole(mix[k], k, (place, y))
-        b_right[k, own] = send(here, here, to_right)
-        b_left[k, own] = send(here, here, to_left)
+        b_along[k, own] = [send(here, here, along_y[at]) for at in (0, 2)]
 
     def finish_mix(k):
-        for h, half in enumerate(HALVES):
-            if half[0] != k:
-                continue
-            z_direct[h].wait_recv()
-            z_sum[h].wait_recv()
-            own, up, down = (
-                part(par[k], half, (0,)),
-                part(zl[k], half, ()),
-                part(zr[k], half, ()),
-            )
-            target = part(mix[k], half, (xh, y))
-
-            def body(i, own=own, up=up, down=down, target=target):
-                rs = tiles16(i)
-                total = own[rs].astype(F32) + up[rs].astype(F32) + down[rs].astype(F32)
-                target[rs] = total.astype(BF16)
-
-            steps(half[3] // 16, body)
+        for copy in z_sums[k]:
+            copy.wait_recv()
+        for mat in range(MATS[k]):
+            terms = [matrix(par[k], k, mat, (0,))]
+            terms += [matrix(za[k], k, mat, (at,)) for at in range(3)]
+            add_up(matrix(mix[k], k, mat, (xh, y)), terms, ROWS[k])
         here = whole(mix[k], k, (xh, y))
         b_far[k] = send(here, here, to_far)
         spread(k, True)
 
-    xo = 1 - xh
-
     def spread_far(k):
         b_far[k].wait_recv()
         spread(k, False)
 
+    b_relay = {}
+
     def relay_mix(k, own):
-        place = xh if own else xo
-        b_right[k, own].wait_recv()
-        b_left[k, own].wait_recv()
-        for h, half in enumerate(HALVES):
-            if half[0] != k:
-                continue
-            step = 3 if half[4] else 1
-            here = part(mix[k], half, (place, (y + step) % 4))
-            b_relay[h, own] = send(here, here, to_right if half[4] else to_left)
-
-    c_first, c_direct, c_sum = {}, {}, {}
+        place = xh if own else 1 - xh
+        for copy in b_along[k, own]:
+            copy.wait_recv()
+        b_relay[k, own] = []
+        for mat, first, rows, up in PARTS[k]:
+            source = matrix(mix[k], k, mat, (place, (y + (3 if up else 1)) % 4))
+            source = source.at[pl.ds(first, rows)]
+            b_relay[k, own].append(send(source, source, along_y[0 if up else 2]))
+
+    v_copies = []
+    c_far = {}
+
+    def send_rows():
+        for k, source in enumerate((v0, v1, v2)):
+            rows = ROWS[k]
+            for at in (0, 2, 1):
+                for side in range(2):
+                    first = (side * 4 + (y + at + 1) % 4) * rows
+                    part = source.at[pl.ds(pl.multiple_of(first, 16), rows)]
+                    v_copies.append(send(part, far_v[k].at[at, side], along_y[at]))
 
     def weight_grads(k):
         rows = ROWS[k]
-        far_rows[k].wait_recv()
-
-        def body(b):
-            own = pl.ds(pl.multiple_of((xh * 4 + b) * rows, 16), rows)
-            far = pl.ds(pl.multiple_of(b * rows, 16), rows)
-            if k == 0:
-                total = contract(v0[own], d0[...], 1, 1) + contract(far_v0[far], p0[...], 1, 1)
-                gw0[b] = (WEIGHT_SCALE * total).astype(BF16)
-            else:
-                v, d, s, p, q = ((v1, d1, s1, p1, q1), (v2, d2, s2, p2, q2))[k - 1]
-                mine, other = v[own], far_v[k][far]
-                real = contract(mine, d[...], 1, 1) + contract(other, p[...], 1, 1)
-                gw[k][0, b] = (WEIGHT_SCALE * real).astype(BF16)
-                imag = contract(mine, s[...], 1, 1) + contract(other, q[...], 1, 1)
-                gw[k][1, b] = (WEIGHT_SCALE * imag).astype(BF16)
-
-        steps(4, body)
-        for h, half in enumerate(HALVES):
-            if half[0] != k:
-                continue
-
-            def block(step, half=half):
-                return part(gw[k], half, ((y + step) % 4,))
-
-            if half[4]:
-                c_first[h] = send(block(2), part(cf[k], half, ()), to_right)
-                c_direct[h] = send(block(3), part(cr[k], half, ()), to_left)
-            else:
-                c_first[h] = send(block(2), part(cf[k], half, ()), to_left)
-                c_direct[h] = send(block(1), part(cl[k], half, ()), to_right)
-
-    def relay_grads(k):
-        for h, half in enumerate(HALVES):
-            if half[0] != k:
-                continue
-            here = part(gw[k], half, ((y + (1 if half[4] else 3)) % 4,))
-            c_first[h].wait_recv()
-            add_into(here, part(cf[k], half, ()), half[3])
-            target = cl[k] if half[4] else cr[k]
-            c_sum[h] = send(here, part(target, half, ()), to_right if half[4] else to_left)
+        v, d, p = ((v0, d0, p0), (v1, d1, p1), (v2, d2, p2))[k]
+        swapped = (None, (s1, q1), (s2, q2))[k]
+        for mat in range(MATS[k]):
+            near, far = (d, p) if mat == 0 else swapped
+
+            def sums(side):
+                own = v[pl.ds(pl.multiple_of((side * 4 + y) * rows, 16), rows)]
+                total = contract(own, near[...], 1, 1)
+                for at in range(3):
+                    total = total + contract(far_v[k][at, side], far[at], 1, 1)
+                return WEIGHT_SCALE * total
+
+            lead = () if k == 0 else (mat,)
+            cs[k][lead + (slice(None),)] = sums(1 - xh).astype(BF16)
+            keep[k][lead + (slice(None),)] = sums(xh)
+        c_far[k] = send(cs[k], cx[k], to_far)
 
     def finish_grads(k):
-        for h, half in enumerate(HALVES):
-            if half[0] != k:
-                continue
-            c_direct[h].wait_recv()
-            c_sum[h].wait_recv()
-            own, left, right = (
-                part(gw[k], half, (y,)),
-                part(cl[k], half, ()),
-                part(cr[k], half, ()),
-            )
-            target = part(out[k], half, (0,)) if k == 0 else out[k].at[0, half[1]]
-
-            def body(i, own=own, left=left, right=right, target=target):
-                rs = tiles16(i)
-                total = own[rs].astype(F32) + left[rs].astype(F32) + right[rs].astype(F32)
-                target[rs] = total.astype(BF16)
-
-            steps(half[3] // 16, body)
+        c_far[k].wait_recv()
+        for mat in range(MATS[k]):
+            target = out[k].at[(0,) if k == 0 else (0, mat)]
+            add_up(target, [matrix(keep[k], k, mat, ()), matrix(cx[k], k, mat, ())], ROWS[k])
 
     def expand(matrix, target):
         wig32[...] = matrix[0:WIG_READ].astype(F32)
@@ -392,72 +330,78 @@
                         target[rs, EDGES : 2 * EDGES] = result[kept - order]
 
     steps(8, lambda i: rotate_into(i, ((rows_f, v0, v1, v2), (rows_b, d0, d1, d2)), blocks))
-    far_rows = []
-    for k, source in enumerate((v0, v1, v2)):
-        rows = 4 * ROWS[k]
-        half = source.at[pl.ds(pl.multiple_of((1 - xh) * rows, 16), rows)]
-        far_rows.append(send(half, far_v[k], to_far))
-
+    send_rows()
     def swap(source, target):
         target[:, 0:EDGES] = source[:, EDGES : 2 * EDGES]
         target[:, EDGES : 2 * EDGES] = -source[:, 0:EDGES]
 
-    swap(d1, s1)
-    swap(d2, s2)
-    t0[...] = v0[...].T
-    for source, target, swapped in ((v1, t1, u1), (v2, t2, u2)):
-        target[...] = source[...].T
-        swapped[0:EDGES] = -target[EDGES : 2 * EDGES]
-        swapped[EDGES : 2 * EDGES] = target[0:EDGES]
-
-    def far_frame():
-        for copy in far_copies:
+    def turn_frames():
+        swap(d1, s1)
+        swap(d2, s2)
+        t0[...] = v0[...].T
+        for source, target, swapped in ((v1, t1, u1), (v2, t2, u2)):
+            target[...] = source[...].T
+            swapped[0:EDGES] = -target[EDGES : 2 * EDGES]
+            swapped[EDGES : 2 * EDGES] = target[0:EDGES]
+
+    def far_frame(at):
+        if at == 1:
+            for copy in arrivals[1]:
+                copy.wait_recv()
+        expand(far_wigner.at[at], far_blocks)
+        hot = far_hot[at]
+
+        def far_gather(i):
+            rows_p[wide(i)] = contract(far_grad[at, :, wide(i)], hot, 0, 0).astype(BF16)
+
+        steps(7, far_gather)
+        frame = (rows_p, p0.at[at], p1.at[at], p2.at[at])
+        steps(8, lambda i: rotate_into(i, (frame,), far_blocks))
+        swap(p1.at[at], q1.at[at])
+        swap(p2.at[at], q2.at[at])
+
+    arrivals = {0: grad_copies[0:3], 2: grad_copies[3:6], 1: []}
+
+    def relay_targets():
+        for copy in grad_copies:
             copy.wait_recv()
-        expand(far_wigner, far_blocks)
-        hot = far_hot[...]
-
-        def far_gather(i):
-            rows_p[wide(i)] = contract(far_grad[:, wide(i)], hot, 0, 0).astype(BF16)
-
-        steps(7, far_gather)
-        steps(8, lambda i: rotate_into(i, ((rows_p, p0, p1, p2),), far_blocks))
-        swap(p1, q1)
-        swap(p2, q2)
+        for ref, rows in ((far_grad, ATOMS // 2), (far_wigner, WIG_READ // 2), (far_hot, ATOMS // 2)):
+            for at, first in ((0, 0), (2, rows)):
+                source, target = (ref.at[i, pl.ds(first, rows)] for i in (at, 1))
+                arrivals[1].append(send(source, target, along_y[at]))
 
     forward_raw(0)
     partials(0)
-    far_frame()
-    relay_sums(0)
+    relay_targets()
+    far_frame(0)
     finish_mix(0)
+    turn_frames()
     forward_raw(1)
-    weight_grads(0)
     partials(1)
     spread_far(0)
     relay_mix(0, True)
-    relay_sums(1)
+    far_frame(2)
     relay_mix(0, False)
+    forward_raw(2)
+    partials(2)
+    far_frame(1)
     finish_mix(1)
-    forward_raw(2)
-    weight_grads(1)
-    partials(2)
+    for copy in v_copies:
+        copy.wait_recv()
+    weight_grads(0)
     spread_far(1)
-    relay_grads(0)
-    relay_sums(2)
     relay_mix(1, True)
     finish_mix(2)
-    weight_grads(2)
+    weight_grads(1)
     relay_mix(1, False)
     spread_far(2)
     relay_mix(2, True)
-    relay_grads(1)
+    weight_grads(2)
     relay_mix(2, False)
-    relay_grads(2)
 
     def convolve(k):
-        for h, half in enumerate(HALVES):
-            if half[0] == k:
-                b_relay[h, True].wait_recv()
-                b_relay[h, False].wait_recv()
+        for copy in b_relay[k, True] + b_relay[k, False]:
+            copy.wait_recv()
         width = COLS[k]
         if k == 0:
             weight = mix0[...].reshape(width, width)
@@ -473,7 +417,7 @@
         result = jnp.dot(real, d[...], preferred_element_type=F32)
         d[...] = (result + jnp.dot(imag, s[...], preferred_element_type=F32)).astype(BF16)
 
-    for copy in far_rows:
+    for copy in v_copies:
         copy.wait_send()
     convolve(0)
     convolve(1)
@@ -544,7 +488,7 @@
         grad_features[:, low:high] = total.astype(BF16)
 
     for copy in copies:
-        if not any(copy is other for other in far_rows):
+        if not any(copy is other for other in v_copies):
             copy.wait_send()
 
 
@@ -552,11 +496,11 @@
     features, grad_out, wigner, sources, targets, ghost_index, edge_count, mixture,
     w_zero, w_one, w_two,
 ):
-    def buffers(*lead):
+    def buffers(*lead, kind=BF16):
         shapes = []
         for k in range(3):
             mats = () if k == 0 else (2,)
-            shapes.append(pltpu.VMEM(mats + lead + (ROWS[k], COLS[k]), BF16))
+            shapes.append(pltpu.VMEM(mats + lead + (ROWS[k], COLS[k]), kind))
         return shapes
 
     raw = [
@@ -566,6 +510,11 @@
         pltpu.VMEM((896, EDGES), BF16),
         pltpu.VMEM((768, 2 * EDGES), BF16),
         pltpu.VMEM((640, 2 * EDGES), BF16),
+    ]
+    far_frames = [
+        pltpu.VMEM((3, 896, EDGES), BF16),
+        pltpu.VMEM((3, 768, 2 * EDGES), BF16),
+        pltpu.VMEM((3, 640, 2 * EDGES), BF16),
     ]
     turned = [
         pltpu.VMEM((EDGES, 896), BF16),
@@ -576,18 +525,18 @@
     scratch = (
         raw
         + buffers(4)
-        + buffers() * 3
+        + buffers(3)
         + buffers(2, 4)
-        + buffers(4)
-        + buffers() * 3
+        + buffers(kind=F32)
+        + buffers() * 2
         + [
-            pltpu.VMEM((ATOMS, WIDTH), BF16),
-            pltpu.VMEM((WIG_READ, EDGES), BF16),
+            pltpu.VMEM((3, ATOMS, WIDTH), BF16),
+            pltpu.VMEM((3, WIG_READ, EDGES), BF16),
             pltpu.VMEM((ATOMS, EDGES), BF16),
-            pltpu.VMEM((ATOMS, EDGES), BF16),
-            pltpu.VMEM((448, EDGES), BF16),
-            pltpu.VMEM((384, 2 * EDGES), BF16),
-            pltpu.VMEM((320, 2 * EDGES), BF16),
+            pltpu.VMEM((3, ATOMS, EDGES), BF16),
+            pltpu.VMEM((3, 2, 112, EDGES), BF16),
+            pltpu.VMEM((3, 2, 96, 2 * EDGES), BF16),
+            pltpu.VMEM((3, 2, 80, 2 * EDGES), BF16),
         ]
         + exchange
         + [pltpu.VMEM((WIG_READ, EDGES), F32)]
@@ -598,8 +547,10 @@
         * 2
         + [pltpu.VMEM((ATOMS + 2 * GHOSTS, WIDTH), BF16)]
         + [pltpu.VMEM((WIDTH, EDGES), BF16)] * 3
-        + frame * 3
-        + frame[1:] * 2
+        + frame * 2
+        + far_frames
+        + frame[1:]
+        + far_frames[1:]
         + turned
         + turned[1:]
         + [pltpu.VMEM((ATOMS, WIDTH), F32), pltpu.VMEM((2 * GHOSTS, WIDTH), F32)]

time: 150 us -> 120 us (0.80)
  Pallas kernels: 141 us -> 110 us
    pallas_call x1, Pallas kernels: 141 us -> 110 us  [on_device(): pl.pallas_call(kernel, out_shape=(jax.ShapeDtypeStruct((ATOMS, WIDTH), BF...]
where the time goes in v3:
time: 120 us; the launch traced here: 118 us
  Pallas kernels  110 us (92%)
  local copies, waits for them, and re-layouts  7.59 us (6%)
  between operations  1.31 us (1%)
    pallas_call x1, Pallas kernels, on_device(): pl.pallas_call(kernel, out_shape=(jax.ShapeDtypeStruct((ATOMS, WIDTH), BF...  110 us
    unnamed x15, local copies, waits for them, and re-layouts  6.33 us

profile of v3, /device:TPU:0, one launch (start us, length us, event | category | flops | bytes accessed | tf_op | source)
XLA Modules:
  0.0 118.5 jit_solution(5806845939111855208)
XLA Ops:
  1.3 0.0 copy-start.4
  1.3 0.7 copy-done.4
  2.0 0.6 reshape.25.ghost_row
  2.5 0.7 reshape.26.ghost_col
  3.2 109.6 %message_layer.1 = (bf16[32,6272]{1,0:T(8,128)(2,1)}, bf16[32,6272]{1,0:T(8,128)(2,1)}, bf16[1,112,896]{2,1,0:T(8,128)(2,1)}, bf16[1,2,96,768]{3,2,1,0:T(8,128)(2,1)}, bf16[1,2,80,640]{3,2,1,0:T(8,128)(2,1)}) custom-call(f32[16,32]{1,0:T(8,128)} %mixture.1, s32[1,1]{1,0:T(1,128)S(6)} %copy.22.count, bf16[32,6272]{1,0:T(8,128)(2,1)} %features.1, ...), custom_call_target="tpu_custom_call" | custom-call | tf_op jit(solution)/shard_map/message_layer/pallas_call | solution.py:561
  112.8 0.0 copy-start
  112.8 1.8 %copy.23 = bf16[32,6272]{1,0:T(8,128)(2,1)} copy(bf16[32,6272]{1,0:T(8,128)(2,1)} %get-tuple-element.10) | data formatting | bytes 802816
  114.7 0.0 copy-done
  114.7 0.0 copy-start.3
  114.7 0.7 copy.24
  115.4 0.3 copy-done.3
  115.7 0.0 copy-start.1
  115.7 0.7 copy.25
  116.4 0.4 copy-done.1
  116.8 0.0 copy-start.2
  116.8 0.7 copy.26
  117.5 0.3 copy-done.2
  117.8 0.7 copy.27
Async XLA Ops:
  1.3 0.7 copy-start.4
  112.8 1.8 %copy-start = (bf16[32,6272]{1,0:T(8,128)(2,1)S(1)}, bf16[32,6272]{1,0:T(8,128)(2,1)}, u32[]{:S(2)}) copy-start(bf16[32,6272]{1,0:T(8,128)(2,1)} %get-tuple-element.11) | copy-start | bytes 1204228
  114.7 1.1 copy-start.3
  115.7 1.0 copy-start.1
  116.8 1.0 copy-start.2

commit v4 on v3

--- a/solution.py
+++ b/solution.py
@@ -25,12 +25,15 @@
 ROWS = (112, 96, 80)
 COLS = (896, 768, 640)
 MATS = (1, 2, 2)
-PARTS = (
-    ((0, 0, 48, True), (0, 48, 64, False)),
-    ((0, 0, 96, True), (1, 0, 96, False)),
-    ((0, 0, 80, True), (1, 0, 80, False)),
+PIECES = (
+    (0, 0, 0, 48, 32),
+    (0, 0, 48, 64, 32),
+    (1, 0, 0, 96, 48),
+    (1, 1, 0, 96, 48),
+    (2, 0, 0, 80, 32),
+    (2, 1, 0, 80, 48),
 )
-COPIES = 128
+COPIES = 192
 
 
 def contract(left, right, left_dim, right_dim):
@@ -39,8 +42,16 @@
     )
 
 
-def whole(ref, chunk, lead):
-    return ref.at[lead] if chunk == 0 else ref.at[(slice(None),) + lead]
+def view(ref, piece, lead, first=0, rows=None):
+    k, mat, start, length, _ = piece
+    rs = pl.ds(start + first, length if rows is None else rows)
+    return ref.at[lead + (rs,)] if k == 0 else ref.at[(mat,) + lead + (rs,)]
+
+
+def experts(ref, piece, lead=()):
+    k, mat, start, length, _ = piece
+    lead = lead + (slice(None),)
+    return ref.at[lead + (pl.ds(start, length),)] if k == 0 else ref.at[lead + (mat,)]
 
 
 def steps(count, body):
@@ -56,7 +67,7 @@
 
 
 def kernel(
-    mixture, count, features, grad_out, wigner, sources, targets, ghost_col, ghost_row, w0, w1, w2,
+    mixture, count, features, grad_out, wigner, sources, targets, ghost_index, w0, w1, w2,
     updated, grad_features, out0, out1, out2,
     raw0, raw1, raw2, par0, par1, par2, za0, za1, za2, mix0, mix1, mix2,
     keep0, keep1, keep2, cs0, cs1, cs2, cx0, cx1, cx2,
@@ -118,9 +129,12 @@
         copies.append(copy)
         return copy
 
-    atom_lane = lax.broadcasted_iota(jnp.int32, (2 * GHOSTS, ATOMS), 1)
-    pick = (atom_lane == ghost_col[...]).astype(BF16)
-    ghosts = jnp.dot(pick, features[...], preferred_element_type=F32)
+    atom = lax.broadcasted_iota(jnp.int32, (ATOMS, GHOSTS), 0)
+    spots = jnp.concatenate(
+        [(atom == ghost_index[0, side : side + 1]).astype(F32) for side in range(2)], 1
+    )
+    ghosts = jnp.dot(spots.T.astype(BF16), features[...], preferred_element_type=F32)
+    spots = spots.astype(BF16)
     for side in range(2):
         mine = ghosts[side * GHOSTS : (side + 1) * GHOSTS]
         ghost_send[side] = jnp.concatenate([mine[:, :PACK], mine[:, WIDTH - PACK :]], 0).astype(BF16)
@@ -145,10 +159,11 @@
     ]
     raw_x, raw_core, raw_xc = {}, {}, {}
     grad_copies = []
-    for k in range(3):
-        raw_x[k] = send(w[k], raw[k].at[1], to_x)
-        raw_core[k] = send(w[k], raw[k].at[0], to_core)
-        if k == 0:
+    for i, piece in enumerate(PIECES):
+        k = piece[0]
+        raw_x[i] = send(experts(w[k], piece), experts(raw[k], piece, (1,)), to_x)
+        raw_core[i] = send(experts(w[k], piece), experts(raw[k], piece, (0,)), to_core)
+        if i == 0:
             for at in (0, 2):
                 grad_copies += [
                     send(grad_out, far_grad.at[at], along_y[at]),
@@ -156,15 +171,19 @@
                     send(hot_send, far_hot.at[at], along_y[at]),
                 ]
 
-    def forward_raw(k):
-        raw_x[k].wait_recv()
-        raw_xc[k] = send(raw[k].at[1], raw[k].at[2], to_core)
+    def forward_raw(i):
+        piece = PIECES[i]
+        raw_x[i].wait_recv()
+        here = raw[piece[0]]
+        raw_xc[i] = send(experts(here, piece, (1,)), experts(here, piece, (2,)), to_core)
 
     z_sums = {}
 
-    def partials(k):
-        raw_core[k].wait_recv()
-        raw_xc[k].wait_recv()
+    def partials(i):
+        piece = PIECES[i]
+        k, mat, start, length, _ = piece
+        raw_core[i].wait_recv()
+        raw_xc[i].wait_recv()
         across = COLS[k] // 128
         scale = [
             [
@@ -174,24 +193,24 @@
             ]
             for step in range(4)
         ]
-        for mat in range(MATS[k]):
-            lead = () if k == 0 else (mat,)
-
-            def body(t, mat=mat, lead=lead):
-                rs = tiles16(t // across)
-                c = pl.ds(pl.multiple_of((t % across) * 128, 128), 128)
-                terms = [w[k][(i,) + lead + (rs, c)].astype(F32) for i in range(2)]
-                for slot in range(3):
-                    terms += [raw[k][(slot, i) + lead + (rs, c)].astype(F32) for i in range(2)]
-                for step in range(4):
-                    total = scale[step][0] * terms[0]
-                    for factor, term in zip(scale[step][1:], terms[1:]):
-                        total = total + factor * term
-                    par[k][lead + (step, rs, c)] = total.astype(BF16)
-
-            steps(ROWS[k] // 16 * across, body)
-        z_sums[k] = [
-            send(whole(par[k], k, (at + 1,)), whole(za[k], k, (at,)), along_z[at]) for at in (0, 2, 1)
+        lead = () if k == 0 else (mat,)
+
+        def body(t):
+            rs = pl.ds(pl.multiple_of(start + t // across * 16, 16), 16)
+            c = pl.ds(pl.multiple_of((t % across) * 128, 128), 128)
+            terms = [w[k][(i,) + lead + (rs, c)].astype(F32) for i in range(2)]
+            for slot in range(3):
+                terms += [raw[k][(slot, i) + lead + (rs, c)].astype(F32) for i in range(2)]
+            for step in range(4):
+                total = scale[step][0] * terms[0]
+                for factor, term in zip(scale[step][1:], terms[1:]):
+                    total = total + factor * term
+                par[k][lead + (step, rs, c)] = total.astype(BF16)
+
+        steps(length // 16 * across, body)
+        z_sums[i] = [
+            send(view(par[k], piece, (at + 1,)), view(za[k], piece, (at,)), along_z[at])
+            for at in (0, 2, 1)
         ]
 
     def add_up(target, terms, rows, kind=BF16):
@@ -209,37 +228,38 @@
 
     b_far, b_along = {}, {}
 
-    def spread(k, own):
+    def spread(i, own):
+        piece = PIECES[i]
+        here = view(mix[piece[0]], piece, (xh if own else 1 - xh, y))
+        b_along[i, own] = [send(here, here, along_y[at]) for at in (0, 2)]
+
+    def finish_mix(i):
+        piece = PIECES[i]
+        k = piece[0]
+        for copy in z_sums[i]:
+            copy.wait_recv()
+        here = view(mix[k], piece, (xh, y))
+        terms = [view(par[k], piece, (0,))] + [view(za[k], piece, (at,)) for at in range(3)]
+        add_up(here, terms, piece[3])
+        b_far[i] = send(here, here, to_far)
+        spread(i, True)
+
+    def spread_far(i):
+        b_far[i].wait_recv()
+        spread(i, False)
+
+    b_relay = {}
+
+    def relay_mix(i, own):
+        piece = PIECES[i]
+        k, _, _, length, upward = piece
         place = xh if own else 1 - xh
-        here = whole(mix[k], k, (place, y))
-        b_along[k, own] = [send(here, here, along_y[at]) for at in (0, 2)]
-
-    def finish_mix(k):
-        for copy in z_sums[k]:
+        b_relay[i, own] = []
+        for copy in b_along[i, own]:
             copy.wait_recv()
-        for mat in range(MATS[k]):
-            terms = [matrix(par[k], k, mat, (0,))]
-            terms += [matrix(za[k], k, mat, (at,)) for at in range(3)]
-            add_up(matrix(mix[k], k, mat, (xh, y)), terms, ROWS[k])
-        here = whole(mix[k], k, (xh, y))
-        b_far[k] = send(here, here, to_far)
-        spread(k, True)
-
-    def spread_far(k):
-        b_far[k].wait_recv()
-        spread(k, False)
-
-    b_relay = {}
-
-    def relay_mix(k, own):
-        place = xh if own else 1 - xh
-        for copy in b_along[k, own]:
-            copy.wait_recv()
-        b_relay[k, own] = []
-        for mat, first, rows, up in PARTS[k]:
-            source = matrix(mix[k], k, mat, (place, (y + (3 if up else 1)) % 4))
-            source = source.at[pl.ds(first, rows)]
-            b_relay[k, own].append(send(source, source, along_y[0 if up else 2]))
+        for at, step, first, rows in ((0, 3, 0, upward), (2, 1, upward, length - upward)):
+            here = view(mix[k], piece, (place, (y + step) % 4), first, rows)
+            b_relay[i, own].append(send(here, here, along_y[at]))
 
     v_copies = []
     c_far = {}
@@ -329,6 +349,8 @@
                         target[rs, 0:EDGES] = result[kept + order]
                         target[rs, EDGES : 2 * EDGES] = result[kept - order]
 
+    forward_raw(0)
+    partials(0)
     steps(8, lambda i: rotate_into(i, ((rows_f, v0, v1, v2), (rows_b, d0, d1, d2)), blocks))
     send_rows()
     def swap(source, target):
@@ -370,38 +392,56 @@
                 source, target = (ref.at[i, pl.ds(first, rows)] for i in (at, 1))
                 arrivals[1].append(send(source, target, along_y[at]))
 
-    forward_raw(0)
-    partials(0)
+    forward_raw(1)
     relay_targets()
+    partials(1)
     far_frame(0)
     finish_mix(0)
-    turn_frames()
-    forward_raw(1)
-    partials(1)
-    spread_far(0)
-    relay_mix(0, True)
-    far_frame(2)
-    relay_mix(0, False)
     forward_raw(2)
     partials(2)
+    spread_far(0)
+    finish_mix(1)
+    relay_mix(0, True)
+    turn_frames()
+    forward_raw(3)
+    partials(3)
+    relay_mix(0, False)
+    spread_far(1)
+    finish_mix(2)
+    relay_mix(1, True)
+    far_frame(2)
+    forward_raw(4)
+    partials(4)
+    relay_mix(1, False)
+    spread_far(2)
+    finish_mix(3)
+    relay_mix(2, True)
+    forward_raw(5)
+    partials(5)
     far_frame(1)
-    finish_mix(1)
+    relay_mix(2, False)
+    spread_far(3)
+    finish_mix(4)
+    relay_mix(3, True)
     for copy in v_copies:
         copy.wait_recv()
     weight_grads(0)
-    spread_far(1)
-    relay_mix(1, True)
-    finish_mix(2)
+    finish_mix(5)
+    relay_mix(3, False)
+    spread_far(4)
+    relay_mix(4, True)
     weight_grads(1)
-    relay_mix(1, False)
-    spread_far(2)
-    relay_mix(2, True)
+    spread_far(5)
+    relay_mix(4, False)
+    relay_mix(5, True)
     weight_grads(2)
-    relay_mix(2, False)
+    relay_mix(5, False)
 
     def convolve(k):
-        for copy in b_relay[k, True] + b_relay[k, False]:
-            copy.wait_recv()
+        for i, piece in enumerate(PIECES):
+            if piece[0] == k:
+                for copy in b_relay[i, True] + b_relay[i, False]:
+                    copy.wait_recv()
         width = COLS[k]
         if k == 0:
             weight = mix0[...].reshape(width, width)
@@ -477,9 +517,6 @@
     for copy in back_copies:
         copy.wait_recv()
     came = [back_recv[side].astype(F32) for side in range(2)]
-    spots = (
-        lax.broadcasted_iota(jnp.int32, (ATOMS, 2 * GHOSTS), 0) == ghost_row[...]
-    ).astype(BF16)
     for low, high, first, cut in ((0, PACK, 0, 0), (PACK, WIDTH, GHOSTS, 2 * PACK - WIDTH)):
         both = [a[first : first + GHOSTS, cut : cut + high - low] for a in came]
         both = jnp.concatenate(both, 0).astype(BF16)
@@ -490,6 +527,14 @@
     for copy in copies:
         if not any(copy is other for other in v_copies):
             copy.wait_send()
+
+
+def copy_out(*refs):
+    copies = [pltpu.make_async_copy(refs[i], refs[5 + i], refs[10].at[i]) for i in range(5)]
+    for copy in copies:
+        copy.start()
+    for copy in copies:
+        copy.wait()
 
 
 def on_device(
@@ -558,7 +603,7 @@
     )
     vmem = pl.BlockSpec(memory_space=pltpu.VMEM)
     smem = pl.BlockSpec(memory_space=pltpu.SMEM)
-    return pl.pallas_call(
+    results = pl.pallas_call(
         kernel,
         out_shape=(
             jax.ShapeDtypeStruct((ATOMS, WIDTH), BF16),
@@ -567,7 +612,7 @@
             jax.ShapeDtypeStruct((1, 2, 96, 768), BF16),
             jax.ShapeDtypeStruct((1, 2, 80, 640), BF16),
         ),
-        in_specs=[smem, smem] + [vmem] * 10,
+        in_specs=[smem, smem] + [vmem] * 9,
         out_specs=(vmem,) * 5,
         scratch_shapes=scratch,
         compiler_params=pltpu.CompilerParams(
@@ -582,12 +627,20 @@
         wigner,
         sources.reshape(1, -1),
         targets.reshape(1, -1),
-        ghost_index.reshape(-1, 1),
-        ghost_index.reshape(1, -1),
+        ghost_index,
         w_zero,
         w_one,
         w_two,
     )
+    anywhere = pl.BlockSpec(memory_space=pl.ANY)
+    return pl.pallas_call(
+        copy_out,
+        out_shape=tuple(jax.ShapeDtypeStruct(a.shape, a.dtype) for a in results),
+        in_specs=[vmem] * 5,
+        out_specs=(anywhere,) * 5,
+        scratch_shapes=[pltpu.SemaphoreType.DMA((5,))],
+        name="copy_out",
+    )(*results)
 
 
 def solution(mesh):

time: 120 us -> 107 us (0.89); the launches traced: 118 us -> 107 us
  local copies, waits for them, and re-layouts: 7.59 us -> 0 us
  Pallas kernels: 110 us -> 106 us
    unnamed x15 -> x0, local copies, waits for them, and re-layouts: 6.33 us -> none
    pallas_call x1, Pallas kernels: 110 us -> 103 us  [on_device(): pl.pallas_call(kernel, out_shape=(jax.ShapeDtypeStruct((ATOMS, WIDTH), BF...]
    pallas_call x0 -> x1, Pallas kernels: none -> 2.47 us  [on_device(): pl.pallas_call(copy_out, out_shape=tuple((jax.ShapeDtypeStruct(a.shape, a...]
    reshape x2 -> x0, local copies, waits for them, and re-layouts: 1.27 us -> none  [the longest x1 0.68 us: on_device(): ghost_index.reshape(-1, 1)]
where the time goes in v4:
time: 107 us
  Pallas kernels  106 us (99%)
  between operations  1.29 us (1%)
    pallas_call x1, Pallas kernels, on_device(): pl.pallas_call(kernel, out_shape=(jax.ShapeDtypeStruct((ATOMS, WIDTH), BF...  103 us
    pallas_call x1, Pallas kernels, on_device(): pl.pallas_call(copy_out, out_shape=tuple((jax.ShapeDtypeStruct(a.shape, a...  2.47 us

profile of v4, /device:TPU:0, one launch (start us, length us, event | category | flops | bytes accessed | tf_op | source)
XLA Modules:
  0.0 107.2 jit_solution(14242741308359309511)
XLA Ops:
  1.3 103.5 %message_layer.1 = (bf16[32,6272]{1,0:T(8,128)(2,1)}, bf16[32,6272]{1,0:T(8,128)(2,1)}, bf16[1,112,896]{2,1,0:T(8,128)(2,1)}, bf16[1,2,96,768]{3,2,1,0:T(8,128)(2,1)}, bf16[1,2,80,640]{3,2,1,0:T(8,128)(2,1)}) custom-call(f32[16,32]{1,0:T(8,128)} %mixture.1, s32[1,1]{1,0:T(1,128)S(6)} %copy.16.count, bf16[32,6272]{1,0:T(8,128)(2,1)} %features.1, ...), custom_call_target="tpu_custom_call" | custom-call | tf_op jit(solution)/shard_map/message_layer/pallas_call | solution.py:606
  104.7 2.5 %copy_out.1 = (bf16[32,6272]{1,0:T(8,128)(2,1)}, bf16[32,6272]{1,0:T(8,128)(2,1)}, bf16[1,112,896]{2,1,0:T(8,128)(2,1)}, bf16[1,2,96,768]{3,2,1,0:T(8,128)(2,1)}, bf16[1,2,80,640]{3,2,1,0:T(8,128)(2,1)}) custom-call(bf16[32,6272]{1,0:T(8,128)(2,1)} %get-tuple-element.10.refs_0_, bf16[32,6272]{1,0:T(8,128)(2,1)} %get-tuple-element.11.refs_1_, ...), custom_call_target="tpu_custom_call" | custom-call | tf_op jit(solution)/shard_map/copy_out/pallas_call | solution.py:636

commit v5 on v4

--- a/solution.py
+++ b/solution.py
@@ -196,18 +196,19 @@
         lead = () if k == 0 else (mat,)
 
         def body(t):
-            rs = pl.ds(pl.multiple_of(start + t // across * 16, 16), 16)
-            c = pl.ds(pl.multiple_of((t % across) * 128, 128), 128)
-            terms = [w[k][(i,) + lead + (rs, c)].astype(F32) for i in range(2)]
-            for slot in range(3):
-                terms += [raw[k][(slot, i) + lead + (rs, c)].astype(F32) for i in range(2)]
-            for step in range(4):
-                total = scale[step][0] * terms[0]
-                for factor, term in zip(scale[step][1:], terms[1:]):
-                    total = total + factor * term
-                par[k][lead + (step, rs, c)] = total.astype(BF16)
-
-        steps(length // 16 * across, body)
+            rs = pl.ds(pl.multiple_of(start + t * 16, 16), 16)
+            for block in range(across):
+                c = slice(block * 128, (block + 1) * 128)
+                terms = [w[k][(i,) + lead + (rs, c)].astype(F32) for i in range(2)]
+                for slot in range(3):
+                    terms += [raw[k][(slot, i) + lead + (rs, c)].astype(F32) for i in range(2)]
+                for step in range(4):
+                    total = scale[step][0] * terms[0]
+                    for factor, term in zip(scale[step][1:], terms[1:]):
+                        total = total + factor * term
+                    par[k][lead + (step, rs, c)] = total.astype(BF16)
+
+        steps(length // 16, body)
         z_sums[i] = [
             send(view(par[k], piece, (at + 1,)), view(za[k], piece, (at,)), along_z[at])
             for at in (0, 2, 1)
@@ -277,26 +278,25 @@
         rows = ROWS[k]
         v, d, p = ((v0, d0, p0), (v1, d1, p1), (v2, d2, p2))[k]
         swapped = (None, (s1, q1), (s2, q2))[k]
+        own = [v[pl.ds(pl.multiple_of((side * 4 + y) * rows, 16), rows)] for side in range(2)]
+        own = jnp.concatenate(own, 0)
+        others = [far_v[k][at].reshape(2 * rows, own.shape[1]) for at in range(3)]
         for mat in range(MATS[k]):
             near, far = (d, p) if mat == 0 else swapped
-
-            def sums(side):
-                own = v[pl.ds(pl.multiple_of((side * 4 + y) * rows, 16), rows)]
-                total = contract(own, near[...], 1, 1)
-                for at in range(3):
-                    total = total + contract(far_v[k][at, side], far[at], 1, 1)
-                return WEIGHT_SCALE * total
-
-            lead = () if k == 0 else (mat,)
-            cs[k][lead + (slice(None),)] = sums(1 - xh).astype(BF16)
-            keep[k][lead + (slice(None),)] = sums(xh)
+            total = contract(own, near[...], 1, 1)
+            for at in range(3):
+                total = total + contract(others[at], far[at], 1, 1)
+            total = (WEIGHT_SCALE * total).reshape(2, rows, COLS[k])
+            for side in range(2):
+                matrix(keep[k], k, mat, (side,))[...] = total[side]
+            matrix(cs[k], k, mat, ())[...] = matrix(keep[k], k, mat, (1 - xh,))[...].astype(BF16)
         c_far[k] = send(cs[k], cx[k], to_far)
 
     def finish_grads(k):
         c_far[k].wait_recv()
         for mat in range(MATS[k]):
             target = out[k].at[(0,) if k == 0 else (0, mat)]
-            add_up(target, [matrix(keep[k], k, mat, ()), matrix(cx[k], k, mat, ())], ROWS[k])
+            add_up(target, [matrix(keep[k], k, mat, (xh,)), matrix(cx[k], k, mat, ())], ROWS[k])
 
     def expand(matrix, target):
         wig32[...] = matrix[0:WIG_READ].astype(F32)
@@ -310,12 +310,13 @@
     expand(wigner, blocks)
 
     def wide(i):
-        return pl.ds(pl.multiple_of(i * 896, 128), 896)
+        return slice(i * 896, (i + 1) * 896)
 
     def back_gather(i):
         rows_b[wide(i)] = contract(grad_out[:, wide(i)], hot_quarter, 0, 0).astype(BF16)
 
-    steps(7, back_gather)
+    for i in range(7):
+        back_gather(i)
 
     for copy in ghost_copies:
         copy.wait_recv()
@@ -328,7 +329,8 @@
     def gather(i):
         rows_f[wide(i)] = contract(table[:, wide(i)], hot_source, 0, 0).astype(BF16)
 
-    steps(7, gather)
+    for i in range(7):
+        gather(i)
 
     def rotate_into(i, frames, matrices):
         for source, f0, f1, f2 in frames:
@@ -376,7 +378,8 @@
         def far_gather(i):
             rows_p[wide(i)] = contract(far_grad[at, :, wide(i)], hot, 0, 0).astype(BF16)
 
-        steps(7, far_gather)
+        for i in range(7):
+            far_gather(i)
         frame = (rows_p, p0.at[at], p1.at[at], p2.at[at])
         steps(8, lambda i: rotate_into(i, (frame,), far_blocks))
         swap(p1.at[at], q1.at[at])
@@ -393,42 +396,42 @@
                 arrivals[1].append(send(source, target, along_y[at]))
 
     forward_raw(1)
+    partials(1)
     relay_targets()
-    partials(1)
     far_frame(0)
-    finish_mix(0)
     forward_raw(2)
     partials(2)
-    spread_far(0)
-    finish_mix(1)
-    relay_mix(0, True)
-    turn_frames()
+    finish_mix(0)
+    far_frame(2)
     forward_raw(3)
     partials(3)
-    relay_mix(0, False)
-    spread_far(1)
-    finish_mix(2)
-    relay_mix(1, True)
-    far_frame(2)
+    finish_mix(1)
+    spread_far(0)
+    relay_mix(0, True)
     forward_raw(4)
     partials(4)
-    relay_mix(1, False)
-    spread_far(2)
-    finish_mix(3)
-    relay_mix(2, True)
+    finish_mix(2)
+    spread_far(1)
+    relay_mix(0, False)
+    relay_mix(1, True)
     forward_raw(5)
     partials(5)
+    finish_mix(3)
+    spread_far(2)
+    relay_mix(1, False)
+    relay_mix(2, True)
+    turn_frames()
     far_frame(1)
+    finish_mix(4)
+    spread_far(3)
     relay_mix(2, False)
-    spread_far(3)
-    finish_mix(4)
     relay_mix(3, True)
     for copy in v_copies:
         copy.wait_recv()
     weight_grads(0)
     finish_mix(5)
+    spread_far(4)
     relay_mix(3, False)
-    spread_far(4)
     relay_mix(4, True)
     weight_grads(1)
     spread_far(5)
@@ -492,7 +495,8 @@
         table_own[:, wide(i)] = total[0:ATOMS]
         table_ghost[:, wide(i)] = total[ATOMS : ATOMS + 2 * GHOSTS]
 
-    steps(7, scatter_back)
+    for i in range(7):
+        scatter_back(i)
     for side in range(2):
         mine = table_ghost[side * GHOSTS : (side + 1) * GHOSTS]
         back_send[side] = jnp.concatenate([mine[:, :PACK], mine[:, WIDTH - PACK :]], 0).astype(BF16)
@@ -509,7 +513,8 @@
             features[:, wide(i)].astype(F32) + MESSAGE_SCALE * total
         ).astype(BF16)
 
-    steps(7, scatter)
+    for i in range(7):
+        scatter(i)
 
     for k in range(3):
         finish_grads(k)
@@ -572,7 +577,7 @@
         + buffers(4)
         + buffers(3)
         + buffers(2, 4)
-        + buffers(kind=F32)
+        + buffers(2, kind=F32)
         + buffers() * 2
         + [
             pltpu.VMEM((3, ATOMS, WIDTH), BF16),

time: 107 us -> 106 us (level)
  Pallas kernels: 106 us -> 104 us
    pallas_call x1, Pallas kernels: 103 us -> 102 us  [on_device(): pl.pallas_call(kernel, out_shape=(jax.ShapeDtypeStruct((ATOMS, WIDTH), BF...]
where the time goes in v5:
time: 106 us
  Pallas kernels  104 us (98%)
  between operations  1.29 us (1%)
    pallas_call x1, Pallas kernels, on_device(): pl.pallas_call(kernel, out_shape=(jax.ShapeDtypeStruct((ATOMS, WIDTH), BF...  102 us
    pallas_call x1, Pallas kernels, on_device(): pl.pallas_call(copy_out, out_shape=tuple((jax.ShapeDtypeStruct(a.shape, a...  2.47 us

profile of v5, /device:TPU:0, one launch (start us, length us, event | category | flops | bytes accessed | tf_op | source)
XLA Modules:
  0.0 105.5 jit_solution(3245100521010197104)
XLA Ops:
  1.3 101.7 %message_layer.1 = (bf16[32,6272]{1,0:T(8,128)(2,1)}, bf16[32,6272]{1,0:T(8,128)(2,1)}, bf16[1,112,896]{2,1,0:T(8,128)(2,1)}, bf16[1,2,96,768]{3,2,1,0:T(8,128)(2,1)}, bf16[1,2,80,640]{3,2,1,0:T(8,128)(2,1)}) custom-call(f32[16,32]{1,0:T(8,128)} %mixture.1, s32[1,1]{1,0:T(1,128)S(6)} %copy.16.count, bf16[32,6272]{1,0:T(8,128)(2,1)} %features.1, ...), custom_call_target="tpu_custom_call" | custom-call | tf_op jit(solution)/shard_map/message_layer/pallas_call | solution.py:611
  103.0 2.5 %copy_out.1 = (bf16[32,6272]{1,0:T(8,128)(2,1)}, bf16[32,6272]{1,0:T(8,128)(2,1)}, bf16[1,112,896]{2,1,0:T(8,128)(2,1)}, bf16[1,2,96,768]{3,2,1,0:T(8,128)(2,1)}, bf16[1,2,80,640]{3,2,1,0:T(8,128)(2,1)}) custom-call(bf16[32,6272]{1,0:T(8,128)(2,1)} %get-tuple-element.10.refs_0_, bf16[32,6272]{1,0:T(8,128)(2,1)} %get-tuple-element.11.refs_1_, ...), custom_call_target="tpu_custom_call" | custom-call | tf_op jit(solution)/shard_map/copy_out/pallas_call | solution.py:641

commit v6 on v5

--- a/solution.py
+++ b/solution.py
@@ -211,7 +211,7 @@
         steps(length // 16, body)
         z_sums[i] = [
             send(view(par[k], piece, (at + 1,)), view(za[k], piece, (at,)), along_z[at])
-            for at in (0, 2, 1)
+            for at in (1, 0, 2)
         ]
 
     def add_up(target, terms, rows, kind=BF16):

time: 106 us -> 106 us (level)
  no operation moved by 1% of the time
where the time goes in v6:
time: 106 us
  Pallas kernels  104 us (98%)
  between operations  1.29 us (1%)
    pallas_call x1, Pallas kernels, on_device(): pl.pallas_call(kernel, out_shape=(jax.ShapeDtypeStruct((ATOMS, WIDTH), BF...  102 us
    pallas_call x1, Pallas kernels, on_device(): pl.pallas_call(copy_out, out_shape=tuple((jax.ShapeDtypeStruct(a.shape, a...  2.47 us

profile of v6, /device:TPU:0, one launch (start us, length us, event | category | flops | bytes accessed | tf_op | source)
XLA Modules:
  0.0 105.5 jit_solution(12767439230139267665)
XLA Ops:
  1.3 101.7 %message_layer.1 = (bf16[32,6272]{1,0:T(8,128)(2,1)}, bf16[32,6272]{1,0:T(8,128)(2,1)}, bf16[1,112,896]{2,1,0:T(8,128)(2,1)}, bf16[1,2,96,768]{3,2,1,0:T(8,128)(2,1)}, bf16[1,2,80,640]{3,2,1,0:T(8,128)(2,1)}) custom-call(f32[16,32]{1,0:T(8,128)} %mixture.1, s32[1,1]{1,0:T(1,128)S(6)} %copy.16.count, bf16[32,6272]{1,0:T(8,128)(2,1)} %features.1, ...), custom_call_target="tpu_custom_call" | custom-call | tf_op jit(solution)/shard_map/message_layer/pallas_call | solution.py:611
  103.0 2.5 %copy_out.1 = (bf16[32,6272]{1,0:T(8,128)(2,1)}, bf16[32,6272]{1,0:T(8,128)(2,1)}, bf16[1,112,896]{2,1,0:T(8,128)(2,1)}, bf16[1,2,96,768]{3,2,1,0:T(8,128)(2,1)}, bf16[1,2,80,640]{3,2,1,0:T(8,128)(2,1)}) custom-call(bf16[32,6272]{1,0:T(8,128)(2,1)} %get-tuple-element.10.refs_0_, bf16[32,6272]{1,0:T(8,128)(2,1)} %get-tuple-element.11.refs_1_, ...), custom_call_target="tpu_custom_call" | custom-call | tf_op jit(solution)/shard_map/copy_out/pallas_call | solution.py:641
